TPU v7x, 256 devices: a whole 4x4x8 slice. The times are simulated.
256 devices in a mesh: row: 2 (over core), col: 8 (over z), depth: 16 (over y, x).
Axes of the slice: x: 4, y: 4, z: 8, core: 2. Of those that a mesh axis runs over, the one named last changes fastest.
Arguments:
- tokens: bfloat16 [2560, 4096], P(('depth', 'col'), 'row'), may hold values from -6 to 6
- gate_weight: bfloat16 [4096, 14336], P('row', 'col'), may hold values from -0.09375 to 0.09375
- up_weight: bfloat16 [4096, 14336], P('row', 'col'), may hold values from -0.09375 to 0.09375
- down_weight: bfloat16 [14336, 4096], P('col', 'row'), may hold values from -0.046875 to 0.046875
- cotangent: bfloat16 [2560, 4096], P(('depth', 'col'), 'row'), may hold values from -6 to 6
Outputs:
- layer_out: bfloat16 [2560, 4096], P(('depth', 'col'), 'row')
- input_grad: bfloat16 [2560, 4096], P(('depth', 'col'), 'row')
- gate_grad_w: bfloat16 [4096, 14336], P(('row', 'depth'), 'col')
- up_grad_w: bfloat16 [4096, 14336], P(('row', 'depth'), 'col')
- down_grad_w: bfloat16 [14336, 4096], P('col', ('row', 'depth'))
All inputs are finite; a program needn't handle non-finite values.
Results may differ from a plain program's by a relative error of at most 0.0049.
Values may be sent and summed in bfloat16 or wider, within the bound.
No kernel may reach another device: no remote copies, remote signals or barrier semaphores. Data moves between devices by JAX's collectives and lax.ppermute only.
A program may use at most 192 MiB of HBM per device.

v0:
```python
import functools

import jax
import jax.numpy as jnp
from jax import lax
from jax.experimental import pallas as pl
from jax.experimental.pallas import tpu as pltpu
from jax.sharding import PartitionSpec as P

BF = jnp.bfloat16
F32 = jnp.float32
COLS, SIDE, LANES = 8, 4, 128
ALONG_X = [[SIDE * y + x for x in range(SIDE)] for y in range(SIDE)]
ALONG_Y = [[SIDE * y + x for y in range(SIDE)] for x in range(SIDE)]
MIB = 1 << 20


def dot(left, right, dims):
    return lax.dot_general(left, right, (dims, ((), ())), preferred_element_type=F32)


def to_z(value, step):
    return lax.ppermute(value, "col", [(k, (k + step) % COLS) for k in range(COLS)])


def to_x(value, step):
    pairs = [(k, k // SIDE * SIDE + (k + step) % SIDE) for k in range(SIDE * SIDE)]
    return lax.ppermute(value, "depth", pairs)


def to_y(value, step):
    side = SIDE * SIDE
    return lax.ppermute(value, "depth", [(k, (k + SIDE * step) % side) for k in range(side)])


def to_core(value):
    return lax.ppermute(value, "row", [(0, 1), (1, 0)])


def swap(value, groups):
    return lax.all_to_all(
        value, "depth", split_axis=0, concat_axis=0, axis_index_groups=groups, tiled=True
    )


def shape(*dims, dtype=BF):
    return jax.ShapeDtypeStruct(dims, dtype)


def call(kernel, outs, *args, limit=32, scratch=()):
    return pl.pallas_call(
        kernel,
        out_shape=outs,
        scratch_shapes=list(scratch),
        compiler_params=pltpu.CompilerParams(vmem_limit_bytes=limit * MIB),
    )(*args)


def assemble_kernel(*refs):
    blocks, (feat, upst, send_a, send_b, feat32, upst32) = refs[: COLS + 1], refs[COLS + 1 :]
    rows = blocks[0].shape[0] // 2
    width = feat.shape[1]
    for k in range(COLS):
        if k < COLS // 2:
            block = blocks[k][...].astype(F32)
        elif k == COLS // 2:
            block = jnp.concatenate([blocks[k][...], blocks[k + 1][...]], axis=1).astype(F32)
        else:
            block = blocks[k + 1][...].astype(F32)
        feat32[pl.ds(rows * k, rows), :] = block[:rows]
        upst32[pl.ds(rows * k, rows), :] = block[rows:]
    feat[...] = feat32[...].astype(BF)
    upst[...] = upst32[...].astype(BF)
    quarter = width // SIDE
    for i in range(SIDE):
        send_b[i] = feat[:, quarter * i : quarter * (i + 1)]
        for j in range(SIDE):
            column = LANES * (SIDE * j + i)
            send_a[i, :, LANES * j : LANES * (j + 1)] = feat[:, column : column + LANES]
            send_a[i, :, quarter + LANES * j : quarter + LANES * (j + 1)] = upst[
                :, column : column + LANES
            ]


def gather_col(value):
    half = value.shape[1] // 2
    before, after = to_z(value, 1), to_z(value, -1)
    before2, after2 = to_z(value, 2), to_z(value, -2)
    before3, after3 = to_z(before2, 1), to_z(after2, -1)
    far = (to_z(before2[:, :half], 2), to_z(after2[:, half:], -2))
    return [value, after, after2, after3, *far, before3, before2, before]


def project_kernel(which, feat, upst, gate, up, down, out):
    width = gate.shape[1]
    products = (
        dot(feat[...], gate[...], ((1,), (0,))),
        dot(feat[...], up[...], ((1,), (0,))),
        dot(upst[...], down[...], ((1,), (1,))),
    )
    for k, product in enumerate(products):
        place = (slice(None), slice(width * k, width * (k + 1)))

        @pl.when(pl.program_id(0) == 0)
        def _():
            out[place] = product

        @pl.when(pl.program_id(0) != 0)
        def _():
            out[place] = out[place] + product


def project(which, features, upstream, gate_weight, up_weight, down_weight):
    group, model = features.shape
    half = gate_weight.shape[1] // 2
    step = model // 4
    return pl.pallas_call(
        project_kernel,
        grid_spec=pltpu.PrefetchScalarGridSpec(
            num_scalar_prefetch=1,
            grid=(model // step,),
            in_specs=[
                pl.BlockSpec((group, step), lambda k, w: (0, k)),
                pl.BlockSpec((group, step), lambda k, w: (0, k)),
                pl.BlockSpec((step, half), lambda k, w: (k, w[0])),
                pl.BlockSpec((step, half), lambda k, w: (k, w[0])),
                pl.BlockSpec((half, step), lambda k, w: (w[0], k)),
            ],
            out_specs=pl.BlockSpec((group, 3 * half), lambda k, w: (0, 0)),
        ),
        out_shape=shape(group, 3 * half, dtype=F32),
        compiler_params=pltpu.CompilerParams(vmem_limit_bytes=24 * MIB),
    )(which, features, upstream, gate_weight, up_weight, down_weight)


def swiglu_kernel(own, theirs, route_a, route_b):
    half = own.shape[1] // 3
    cut = route_a.shape[1] - half
    parts = [slice(half * k, half * (k + 1)) for k in range(3)]
    gate_pre = own[:, parts[0]] + theirs[:, parts[0]]
    up_pre = own[:, parts[1]] + theirs[:, parts[1]]
    hidden_grad = own[:, parts[2]] + theirs[:, parts[2]]
    logistic = jax.nn.sigmoid(gate_pre)
    route_a[:, :half] = (gate_pre * logistic * up_pre).astype(BF)
    gate_grad = hidden_grad * up_pre * logistic * (1.0 + gate_pre * (1.0 - logistic))
    gate_grad = gate_grad.astype(BF)
    route_a[:, half:] = gate_grad[:, :cut]
    route_b[:, : half - cut] = gate_grad[:, cut:]
    route_b[:, half - cut :] = (hidden_grad * gate_pre * logistic).astype(BF)


def back_kernel(place, a_own, b_own, a_theirs, b_theirs, down, gate, up, out, inp, total):
    half = down.shape[0]
    cut = a_own.shape[1] - half
    rest = half - cut
    rows = out.shape[1]
    inner = pl.program_id(1)

    def add(a, b):
        grads = jnp.concatenate([a[:, half:], b[:, :rest]], axis=1)
        first = dot(a[:, :half], down[...], ((1,), (0,)))
        second = dot(grads, gate[...], ((1,), (1,))) + dot(b[:, rest:], up[...], ((1,), (1,)))
        return first, second

    @pl.when(inner == 0)
    def _():
        total[0], total[1] = add(a_own, b_own)

    @pl.when(inner == 1)
    def _():
        first, second = add(a_theirs, b_theirs)
        first = total[0] + first
        second = total[1] + second
        for k in range(COLS):
            at = lax.rem(place[1] + k, COLS)
            out[at] = first[rows * k : rows * (k + 1)].astype(BF)
            inp[at] = second[rows * k : rows * (k + 1)].astype(BF)


def back(place, routes, down_weight, gate_weight, up_weight, rows):
    units, model = down_weight.shape
    half = units // 2
    step = model // 4

    def whole(value):
        return pl.BlockSpec(value.shape, lambda n, j, p: (0, 0))

    def pick(j, p):
        return lax.rem(p[0] + j, 2)

    block = pl.BlockSpec((COLS, rows, step), lambda n, j, p: (0, 0, n))
    return pl.pallas_call(
        back_kernel,
        grid_spec=pltpu.PrefetchScalarGridSpec(
            num_scalar_prefetch=1,
            grid=(model // step, 2),
            in_specs=[whole(r) for r in routes]
            + [
                pl.BlockSpec((half, step), lambda n, j, p: (pick(j, p), n)),
                pl.BlockSpec((step, half), lambda n, j, p: (n, pick(j, p))),
                pl.BlockSpec((step, half), lambda n, j, p: (n, pick(j, p))),
            ],
            out_specs=[block, block],
            scratch_shapes=[pltpu.VMEM((2, COLS * rows, step), F32)],
        ),
        out_shape=[shape(COLS, rows, model)] * 2,
        compiler_params=pltpu.CompilerParams(vmem_limit_bytes=24 * MIB),
    )(place, *routes, down_weight, gate_weight, up_weight)


def weight_kernel(cut, place, *refs):
    pieces, columns = refs[:4], refs[4:6]
    own, before, after, far_a, far_b, total = refs[6:]
    width = SIDE * LANES
    for t in range(2):
        for s, (piece, offset) in enumerate(zip(pieces, (0, SIDE - 1, 1, 2))):
            rows = columns[t][lax.rem(place[0] + offset, SIDE)]
            part = dot(rows[:, :width], piece[:, cut:], ((0,), (0,)))
            total[:, cut:] = part if s == 0 else total[:, cut:] + part
            if cut:
                part = dot(rows[:, width:], piece[:, :cut], ((0,), (0,)))
                total[:, :cut] = part if s == 0 else total[:, :cut] + part
        here = pl.ds(LANES * t, LANES)
        for ref, offset in ((own, 0), (before, SIDE - 1), (after, 1), ((far_a, far_b)[t], 2)):
            start = pl.multiple_of(LANES * lax.rem(place[1] + offset, SIDE), LANES)
            value = total[pl.ds(start, LANES), :]
            if ref is far_a or ref is far_b:
                ref[...] = value.astype(BF)
            else:
                ref[here, :] = value


def weight_partials(cut, place, pieces, columns):
    wide = pieces[0].shape[1]
    vmem = pl.BlockSpec(memory_space=pltpu.VMEM)
    return pl.pallas_call(
        functools.partial(weight_kernel, cut),
        in_specs=[pl.BlockSpec(memory_space=pltpu.SMEM)] + [vmem] * 6,
        out_specs=[vmem] * 5,
        out_shape=[shape(2 * LANES, wide, dtype=F32)] * 3 + [shape(LANES, wide)] * 2,
        scratch_shapes=[pltpu.VMEM((SIDE * LANES, wide), F32)],
        compiler_params=pltpu.CompilerParams(vmem_limit_bytes=32 * MIB),
    )(place, *pieces, *columns)


def pass_on_kernel(before, after, from_before, from_after, send_before, send_after):
    first, second = pl.ds(0, LANES), pl.ds(LANES, LANES)
    send_after[first, :] = (after[first, :] + from_before[...].astype(F32)).astype(BF)
    send_after[second, :] = after[second, :].astype(BF)
    send_before[first, :] = before[first, :].astype(BF)
    send_before[second, :] = (before[second, :] + from_after[...].astype(F32)).astype(BF)


def sum_kernel(own, from_before, from_after, mine, theirs):
    total = own[...] + from_before[...].astype(F32) + from_after[...].astype(F32)
    mine[...] = total[:LANES].astype(BF)
    theirs[...] = total[LANES:].astype(BF)


def scatter(parts, send):
    own, before, after, far_a, far_b = parts
    wide = own.shape[1]
    from_before, from_after = send(far_a, 1), send(far_b, -1)
    pair = [shape(2 * LANES, wide)] * 2
    send_before, send_after = call(pass_on_kernel, pair, before, after, from_before, from_after)
    from_before, from_after = send(send_after, 1), send(send_before, -1)
    pair = [shape(LANES, wide)] * 2
    return call(sum_kernel, pair, own, from_before, from_after)


def gather(value, send):
    before, after = send(value, 1), send(value, -1)
    return [value, before, after, send(before, 1)]


def body(tokens, gate_weight, up_weight, down_weight, cotangent):
    row, col, depth = (lax.axis_index(name) for name in ("row", "col", "depth"))
    first = row == 0
    at_x, at_y = depth % SIDE, depth // SIDE
    rows, model = tokens.shape
    group = rows * COLS
    half = gate_weight.shape[1] // 2
    cut = (half // LANES // 2 + 1) * LANES
    width = SIDE * LANES

    blocks = gather_col(jnp.concatenate([tokens, cotangent], axis=0))
    features, upstream, send_a, send_b = call(
        assemble_kernel,
        [
            shape(group, model),
            shape(group, model),
            shape(SIDE, group, 2 * width),
            shape(SIDE, group, width),
        ],
        *blocks,
        scratch=[pltpu.VMEM((group, model), F32)] * 2,
    )
    weights = (gate_weight, up_weight, down_weight)
    sent = project(jnp.reshape(1 - row, (1,)), features, upstream, *weights)
    kept = project(jnp.reshape(row, (1,)), features, upstream, *weights)
    routes = call(
        swiglu_kernel,
        [shape(group, half + cut), shape(group, 2 * half - cut)],
        kept,
        to_core(sent),
    )
    route_a, route_b = routes

    columns_a = swap(send_a, ALONG_X)
    columns_b = swap(send_b, ALONG_Y)
    columns_a = (columns_a, to_core(columns_a))
    columns_b = (columns_b, to_core(columns_b))

    wide_a = gather(route_a, to_x)
    wide_b = gather(route_b, to_y)

    theirs = (to_core(route_a), to_core(route_b))
    out_part, in_part = back(
        jnp.stack([row, col]),
        (route_a, route_b, *theirs),
        down_weight,
        gate_weight,
        up_weight,
        rows,
    )

    part_a = weight_partials(half, jnp.stack([at_x, at_y]), wide_a, columns_a)
    part_b = weight_partials(0, jnp.stack([at_y, at_x]), wide_b, columns_b)
    mine_a, other_a = scatter(part_a, to_y)
    mine_b, other_b = scatter(part_b, to_x)
    other_a, other_b = to_core(other_a), to_core(other_b)
    rest = half - cut

    def both(own, theirs):
        return jnp.concatenate(
            [jnp.where(first, own, theirs), jnp.where(first, theirs, own)], axis=1
        )

    def gate_of(a, b):
        return jnp.concatenate([a[:, half:], b[:, :rest]], axis=1)

    gate_grad_w = both(gate_of(mine_a, mine_b), gate_of(other_a, other_b))
    up_grad_w = both(mine_b[:, rest:], other_b[:, rest:])
    down_grad_w = both(mine_a[:, :half], other_a[:, :half]).T

    part = jnp.concatenate([out_part, in_part], axis=2)
    moved = lax.all_to_all(part, "col", split_axis=0, concat_axis=0, tiled=True)
    total = jnp.sum(moved.astype(F32), axis=0).astype(BF)
    return (total[:, :model], total[:, model:], gate_grad_w, up_grad_w, down_grad_w)


def solution(mesh):
    in_specs = (
        P(("depth", "col"), "row"),
        P("row", "col"),
        P("row", "col"),
        P("col", "row"),
        P(("depth", "col"), "row"),
    )
    out_specs = (
        P(("depth", "col"), "row"),
        P(("depth", "col"), "row"),
        P(("row", "depth"), "col"),
        P(("row", "depth"), "col"),
        P("col", ("row", "depth")),
    )
    return jax.shard_map(body, mesh=mesh, in_specs=in_specs, out_specs=out_specs, check_vma=False)
```

profile of v0, /device:TPU:1, one launch (start us, length us, event | category | flops | bytes accessed | tf_op | source)
XLA Modules:
  0.0 201.4 jit_solution(4233343151945688222)
XLA Ops:
  1.6 6.9 %collective-permute-start.1 = (bf16[40,2048]{1,0:T(8,128)(2,1)S(1)}, bf16[40,2048]{1,0:T(8,128)(2,1)S(1)}, u32[]{:S(2)}, u32[]{:S(2)}) collective-permute-start(bf16[40,2048]{1,0:T(8,128)(2,1)S(1)} %pad_maximum_fusion.5.refs_0_), channel_id=1, source_target_pairs={{0,96},{16,112},{32,0},{48,16},{64,32},{80,48},{96,64},{112,80},{1... | collective-permute-start | bytes 491528 | tf_op jit(solution)/shard_map/ppermute | solution.py:23
  8.5 3.1 %collective-permute-start = (bf16[40,2048]{1,0:T(8,128)(2,1)S(1)}, bf16[40,2048]{1,0:T(8,128)(2,1)S(1)}, u32[]{:S(2)}, u32[]{:S(2)}) collective-permute-start(bf16[40,2048]{1,0:T(8,128)(2,1)S(1)} %pad_maximum_fusion.5.refs_0_), channel_id=1, source_target_pairs={{0,112},{16,0},{32,16},{48,32},{64,48},{80,64},{96,80},{112,96},{1... | collective-permute-start | bytes 491528 | tf_op jit(solution)/shard_map/ppermute | solution.py:23
  11.7 2.3 %collective-permute-done.1.refs_2_ = bf16[40,2048]{1,0:T(8,128)(2,1)S(1)} collective-permute-done((bf16[40,2048]{1,0:T(8,128)(2,1)S(1)}, bf16[40,2048]{1,0:T(8,128)(2,1)S(1)}, u32[]{:S(2)}, u32[]{:S(2)}) %collective-permute-start.1) | collective-permute-done | bytes 163872 | tf_op jit(solution)/shard_map/ppermute | solution.py:23
  13.9 4.1 %collective-permute-start.2 = (bf16[40,2048]{1,0:T(8,128)(2,1)S(1)}, bf16[40,2048]{1,0:T(8,128)(2,1)S(1)}, u32[]{:S(2)}, u32[]{:S(2)}) collective-permute-start(bf16[40,2048]{1,0:T(8,128)(2,1)S(1)} %collective-permute-done.1.refs_2_), channel_id=1, source_target_pairs={{0,112},{16,0},{32,16},{48,32},{64,48},{80,64},{96,80},{112,96},{1... | collective-permute-start | bytes 491528 | tf_op jit(solution)/shard_map/ppermute | solution.py:23
  18.0 1.5 collective-permute-start.6
  19.6 3.6 %collective-permute-start.5 = (bf16[40,1024]{1,0:T(8,128)(2,1)S(1)}, bf16[40,1024]{1,0:T(8,128)(2,1)S(1)}, u32[]{:S(2)}, u32[]{:S(2)}) collective-permute-start(bf16[40,1024]{1,0:T(8,128)(2,1)S(1)} %slice.49), channel_id=1, source_target_pairs={{0,96},{16,112},{32,0},{48,16},{64,32},{80,48},{96,64},{112,80},{1... | collective-permute-start | bytes 245768 | tf_op jit(solution)/shard_map/ppermute | solution.py:23
  23.3 4.2 %collective-permute-done.4.refs_4_ = bf16[40,1024]{1,0:T(8,128)(2,1)S(1)} collective-permute-done((bf16[40,1024]{1,0:T(8,128)(2,1)S(1)}, bf16[40,1024]{1,0:T(8,128)(2,1)S(1)}, u32[]{:S(2)}, u32[]{:S(2)}) %collective-permute-start.4) | collective-permute-done | bytes 81952 | tf_op jit(solution)/shard_map/ppermute | solution.py:23
  27.5 1.5 shard_map.92
  30.1 4.2 %all-to-all-start.2 = ((bf16[4,160,512]{2,1,0:T(8,128)(2,1)}), bf16[4,160,512]{2,1,0:T(8,128)(2,1)S(1)}, u32[]{:S(2)}, u32[]{:S(2)}) async-start(bf16[4,160,512]{2,1,0:T(8,128)(2,1)} %get-tuple-element.46), calls=%async_computation.2 | async-start | bytes 1310720 | tf_op jit(solution)/shard_map/all_to_all | solution.py:41
  34.3 3.1 %copy-done = bf16[2048,1792]{1,0:T(8,128)(2,1)S(1)} copy-done((bf16[2048,1792]{1,0:T(8,128)(2,1)S(1)}, bf16[2048,1792]{1,0:T(8,128)(2,1)}, u32[]{:S(2)}) %copy-start) | copy-done | bytes 7340056
  37.4 3.1 %copy-done.3 = bf16[2048,1792]{1,0:T(8,128)(2,1)S(1)} copy-done((bf16[2048,1792]{1,0:T(8,128)(2,1)S(1)}, bf16[2048,1792]{1,0:T(8,128)(2,1)}, u32[]{:S(2)}) %copy-start.3) | copy-done | bytes 7340056
  40.5 3.1 %copy-done.6 = bf16[1792,2048]{1,0:T(8,128)(2,1)S(1)} copy-done((bf16[1792,2048]{1,0:T(8,128)(2,1)S(1)}, bf16[1792,2048]{1,0:T(8,128)(2,1)}, u32[]{:S(2)}) %copy-start.6) | copy-done | bytes 7340056
  43.6 6.1 %shard_map.94 = f32[160,2688]{1,0:T(8,128)} custom-call(s32[1]{0:T(128)} %bitcast.2.which, bf16[160,2048]{1,0:T(8,128)(2,1)S(1)} %get-tuple-element.31.feat, bf16[160,2048]{1,0:T(8,128)(2,1)S(1)} %get-tuple-element.32.upst, bf16[2048,1792]{1,0:T(8,128)(2,1)S(1)} %copy-done, bf16[2048,1792]{1,0:T(8,128)(2,1)S(1)} %copy-done.3, bf16[1792,2048]{1,0:T(8,128)(2,1)S(1)} %copy-done.6), custom_call_target="tpu_custom_call" | custom-call | tf_op jit(solution)/shard_map/pallas_call | solution.py:117
  49.6 3.5 %collective-permute-start.8 = (f32[160,2688]{1,0:T(8,128)}, f32[160,2688]{1,0:T(8,128)}, u32[]{:S(2)}, u32[]{:S(2)}) collective-permute-start(f32[160,2688]{1,0:T(8,128)} %shard_map.94), channel_id=1, source_target_pairs={{0,128},{128,0},{1,129},{129,1},{2,130},{130,2},{3,131},{131,3},{4... | collective-permute-start | bytes 5160968 | tf_op jit(solution)/shard_map/ppermute | solution.py:37
  53.2 4.0 %all-to-all-start.1 = ((bf16[4,160,1024]{2,1,0:T(8,128)(2,1)}), bf16[4,160,1024]{2,1,0:T(8,128)(2,1)S(1)}, u32[]{:S(2)}, u32[]{:S(2)}) async-start(bf16[4,160,1024]{2,1,0:T(8,128)(2,1)} %copy-done.19), calls=%async_computation.1 | async-start | bytes 2621440 | tf_op jit(solution)/shard_map/all_to_all | solution.py:41
  57.5 17.5 %all-to-all-done.1.refs_4_ = bf16[4,160,1024]{2,1,0:T(8,128)(2,1)S(1)} async-done(((bf16[4,160,1024]{2,1,0:T(8,128)(2,1)}), bf16[4,160,1024]{2,1,0:T(8,128)(2,1)S(1)}, u32[]{:S(2)}, u32[]{:S(2)}) %all-to-all-start.1) | async-done | bytes 1310752 | tf_op jit(solution)/shard_map/all_to_all | solution.py:41
  76.1 3.1 %copy-done.1 = bf16[2048,1792]{1,0:T(8,128)(2,1)S(1)} copy-done((bf16[2048,1792]{1,0:T(8,128)(2,1)S(1)}, bf16[2048,1792]{1,0:T(8,128)(2,1)}, u32[]{:S(2)}) %copy-start.1) | copy-done | bytes 7340056
  79.1 3.1 %copy-done.4 = bf16[2048,1792]{1,0:T(8,128)(2,1)S(1)} copy-done((bf16[2048,1792]{1,0:T(8,128)(2,1)S(1)}, bf16[2048,1792]{1,0:T(8,128)(2,1)}, u32[]{:S(2)}) %copy-start.4) | copy-done | bytes 7340056
  82.2 3.1 %copy-done.7 = bf16[1792,2048]{1,0:T(8,128)(2,1)S(1)} copy-done((bf16[1792,2048]{1,0:T(8,128)(2,1)S(1)}, bf16[1792,2048]{1,0:T(8,128)(2,1)}, u32[]{:S(2)}) %copy-start.7) | copy-done | bytes 7340056
  85.3 5.0 %shard_map.93.own = f32[160,2688]{1,0:T(8,128)S(1)} custom-call(s32[1]{0:T(128)} %bitcast.which, bf16[160,2048]{1,0:T(8,128)(2,1)S(1)} %get-tuple-element.31.feat, bf16[160,2048]{1,0:T(8,128)(2,1)S(1)} %get-tuple-element.32.upst, bf16[2048,1792]{1,0:T(8,128)(2,1)S(1)} %copy-done.1, bf16[2048,1792]{1,0:T(8,128)(2,1)S(1)} %copy-done.4, ...), custom_call_target="tpu_custom_call" | custom-call | tf_op jit(solution)/shard_map/pallas_call | solution.py:117
  90.3 1.9 shard_map.95
  93.3 1.7 collective-permute-start.19
  95.9 2.4 %collective-permute-start.12 = (bf16[160,1408]{1,0:T(8,128)(2,1)S(1)}, bf16[160,1408]{1,0:T(8,128)(2,1)}, u32[]{:S(2)}, u32[]{:S(2)}) collective-permute-start(bf16[160,1408]{1,0:T(8,128)(2,1)S(1)} %get-tuple-element.33.a_own.refs_0_), channel_id=1, source_target_pairs={{0,3},{1,0},{2,1},{3,2},{4,7},{5,4},{6,5},{7,6},{8,11},{9,8},{10,9... | collective-permute-start | bytes 1351688 | tf_op jit(solution)/shard_map/ppermute | solution.py:28
  98.3 7.5 %collective-permute-done.11.refs_1_ = bf16[160,1408]{1,0:T(8,128)(2,1)S(1)} collective-permute-done((bf16[160,1408]{1,0:T(8,128)(2,1)S(1)}, bf16[160,1408]{1,0:T(8,128)(2,1)S(1)}, u32[]{:S(2)}, u32[]{:S(2)}) %collective-permute-start.11) | collective-permute-done | bytes 450592 | tf_op jit(solution)/shard_map/ppermute | solution.py:28
  106.0 2.7 %collective-permute-start.20 = (bf16[160,1280]{1,0:T(8,128)(2,1)S(1)}, bf16[160,1280]{1,0:T(8,128)(2,1)}, u32[]{:S(2)}, u32[]{:S(2)}) collective-permute-start(bf16[160,1280]{1,0:T(8,128)(2,1)S(1)} %get-tuple-element.34.b_own.refs_0_), channel_id=1, source_target_pairs={{0,12},{1,13},{2,14},{3,15},{4,0},{5,1},{6,2},{7,3},{8,4},{9,5},{1... | collective-permute-start | bytes 1228808 | tf_op jit(solution)/shard_map/ppermute | solution.py:33
  109.8 3.1 %copy-done.2 = bf16[2048,1792]{1,0:T(8,128)(2,1)S(1)} copy-done((bf16[2048,1792]{1,0:T(8,128)(2,1)S(1)}, bf16[2048,1792]{1,0:T(8,128)(2,1)}, u32[]{:S(2)}) %copy-start.2) | copy-done | bytes 7340056
  112.8 3.1 %copy-done.5 = bf16[2048,1792]{1,0:T(8,128)(2,1)S(1)} copy-done((bf16[2048,1792]{1,0:T(8,128)(2,1)S(1)}, bf16[2048,1792]{1,0:T(8,128)(2,1)}, u32[]{:S(2)}) %copy-start.5) | copy-done | bytes 7340056
  115.9 3.1 %copy-done.8 = bf16[1792,2048]{1,0:T(8,128)(2,1)S(1)} copy-done((bf16[1792,2048]{1,0:T(8,128)(2,1)S(1)}, bf16[1792,2048]{1,0:T(8,128)(2,1)}, u32[]{:S(2)}) %copy-start.8) | copy-done | bytes 7340056
  121.0 10.4 %shard_map.96 = (bf16[8,20,2048]{2,1,0:T(8,128)(2,1)S(1)}, bf16[8,20,2048]{2,1,0:T(8,128)(2,1)S(1)}) custom-call(s32[2]{0:T(128)S(1)} %pad_add_fusion.place, bf16[160,1408]{1,0:T(8,128)(2,1)S(1)} %get-tuple-element.33.a_own.refs_0_, bf16[160,1280]{1,0:T(8,128)(2,1)S(1)} %get-tuple-element.34.b_own.refs_0_, bf16[160,1408]{1,0:T(8,128)(2,1)S(1)} %copy-done.23, ...), custom_call_target="tpu_custom_call" | custom-call | tf_op jit(solution)/shard_map/pallas_call | solution.py:192
  131.5 6.1 %shard_map.100 = (f32[256,1280]{1,0:T(8,128)S(1)}, f32[256,1280]{1,0:T(8,128)S(1)}, f32[256,1280]{1,0:T(8,128)S(1)}, bf16[128,1280]{1,0:T(8,128)(2,1)}, bf16[128,1280]{1,0:T(8,128)(2,1)}) custom-call(s32[2]{0:T(128)S(1)} %pad_add_fusion.2.place, bf16[160,1280]{1,0:T(8,128)(2,1)S(1)} %get-tuple-element.34.b_own.refs_0_, ...), custom_call_target="tpu_custom_call" | custom-call | tf_op jit(solution)/shard_map/pallas_call | solution.py:236
  137.6 1.1 copy-done.13
  140.9 2.7 %collective-permute-start.24 = (bf16[128,1280]{1,0:T(8,128)(2,1)}, bf16[128,1280]{1,0:T(8,128)(2,1)}, u32[]{:S(2)}, u32[]{:S(2)}) collective-permute-start(bf16[128,1280]{1,0:T(8,128)(2,1)} %get-tuple-element.51), channel_id=1, source_target_pairs={{0,3},{1,0},{2,1},{3,2},{4,7},{5,4},{6,5},{7,6},{8,11},{9,8},{10,9... | collective-permute-start | bytes 983048 | tf_op jit(solution)/shard_map/ppermute | solution.py:28
  143.6 6.5 %shard_map.97 = (f32[256,1408]{1,0:T(8,128)S(1)}, f32[256,1408]{1,0:T(8,128)S(1)}, f32[256,1408]{1,0:T(8,128)S(1)}, bf16[128,1408]{1,0:T(8,128)(2,1)}, bf16[128,1408]{1,0:T(8,128)(2,1)}) custom-call(s32[2]{0:T(128)S(1)} %pad_add_fusion.1.place, bf16[160,1408]{1,0:T(8,128)(2,1)S(1)} %get-tuple-element.33.a_own.refs_0_, bf16[160,1408]{1,0:T(8,128)(2,1)S(1)} %copy-done.21, ...), custom_call_target="tpu_custom_call" | custom-call | tf_op jit(solution)/shard_map/pallas_call | solution.py:236
  150.1 1.1 copy-done.9
  152.6 2.4 %collective-permute-start.16 = (bf16[128,1408]{1,0:T(8,128)(2,1)}, bf16[128,1408]{1,0:T(8,128)(2,1)}, u32[]{:S(2)}, u32[]{:S(2)}) collective-permute-start(bf16[128,1408]{1,0:T(8,128)(2,1)} %get-tuple-element.42), channel_id=1, source_target_pairs={{0,12},{1,13},{2,14},{3,15},{4,0},{5,1},{6,2},{7,3},{8,4},{9,5},{1... | collective-permute-start | bytes 1081352 | tf_op jit(solution)/shard_map/ppermute | solution.py:33
  155.0 1.3 pad_maximum_fusion
  156.4 4.4 %all-to-all-start = ((bf16[8,20,4096]{2,1,0:T(8,128)(2,1)}), bf16[8,20,4096]{2,1,0:T(8,128)(2,1)}, u32[]{:S(2)}, u32[]{:S(2)}) async-start(bf16[8,20,4096]{2,1,0:T(8,128)(2,1)} %pad_maximum_fusion), calls=%async_computation | async-start | bytes 3145728 | tf_op jit(solution)/shard_map/all_to_all | solution.py:347
  160.8 1.4 collective-permute-done.15.from_before
  162.2 1.5 shard_map.98
  164.3 2.1 %collective-permute-start.18 = (bf16[256,1408]{1,0:T(8,128)(2,1)S(1)}, bf16[256,1408]{1,0:T(8,128)(2,1)S(1)}, u32[]{:S(2)}, u32[]{:S(2)}) collective-permute-start(bf16[256,1408]{1,0:T(8,128)(2,1)S(1)} %get-tuple-element.44), channel_id=1, source_target_pairs={{0,12},{1,13},{2,14},{3,15},{4,0},{5,1},{6,2},{7,3},{8,4},{9,5},{1... | collective-permute-start | bytes 2162696 | tf_op jit(solution)/shard_map/ppermute | solution.py:33
  166.4 1.3 shard_map.101
  167.8 2.7 %collective-permute-start.26 = (bf16[256,1280]{1,0:T(8,128)(2,1)S(1)}, bf16[256,1280]{1,0:T(8,128)(2,1)S(1)}, u32[]{:S(2)}, u32[]{:S(2)}) collective-permute-start(bf16[256,1280]{1,0:T(8,128)(2,1)S(1)} %get-tuple-element.53), channel_id=1, source_target_pairs={{0,3},{1,0},{2,1},{3,2},{4,7},{5,4},{6,5},{7,6},{8,11},{9,8},{10,9... | collective-permute-start | bytes 1966088 | tf_op jit(solution)/shard_map/ppermute | solution.py:28
  170.5 9.6 %collective-permute-done.17.from_before = bf16[256,1408]{1,0:T(8,128)(2,1)S(1)} collective-permute-done((bf16[256,1408]{1,0:T(8,128)(2,1)S(1)}, bf16[256,1408]{1,0:T(8,128)(2,1)S(1)}, u32[]{:S(2)}, u32[]{:S(2)}) %collective-permute-start.17) | collective-permute-done | bytes 720928 | tf_op jit(solution)/shard_map/ppermute | solution.py:33
  180.3 3.5 %collective-permute-start.27 = (bf16[128,1408]{1,0:T(8,128)(2,1)S(1)}, bf16[128,1408]{1,0:T(8,128)(2,1)S(1)}, u32[]{:S(2)}, u32[]{:S(2)}) collective-permute-start(bf16[128,1408]{1,0:T(8,128)(2,1)S(1)} %get-tuple-element.55), channel_id=1, source_target_pairs={{0,128},{128,0},{1,129},{129,1},{2,130},{130,2},{3,131},{131,3},{4... | collective-permute-start | bytes 1081352 | tf_op jit(solution)/shard_map/ppermute | solution.py:37
  184.0 2.4 %collective-permute-start.28 = (bf16[128,1280]{1,0:T(8,128)(2,1)S(1)}, bf16[128,1280]{1,0:T(8,128)(2,1)S(1)}, u32[]{:S(2)}, u32[]{:S(2)}) collective-permute-start(bf16[128,1280]{1,0:T(8,128)(2,1)S(1)} %get-tuple-element.56), channel_id=1, source_target_pairs={{0,128},{128,0},{1,129},{129,1},{2,130},{130,2},{3,131},{131,3},{4... | collective-permute-start | bytes 983048 | tf_op jit(solution)/shard_map/ppermute | solution.py:37
  186.5 1.2 collective-permute-done.28
  190.6 8.4 %all-to-all-done = bf16[8,20,4096]{2,1,0:T(8,128)(2,1)} async-done(((bf16[8,20,4096]{2,1,0:T(8,128)(2,1)}), bf16[8,20,4096]{2,1,0:T(8,128)(2,1)}, u32[]{:S(2)}, u32[]{:S(2)}) %all-to-all-start) | async-done | bytes 1310752 | tf_op jit(solution)/shard_map/all_to_all | solution.py:347
  199.0 1.7 reduce_sum.12
  (98 shorter events, 16.9 us)
Async XLA Ops:
  1.6 12.3 %collective-permute-start.1 = (bf16[40,2048]{1,0:T(8,128)(2,1)S(1)}, bf16[40,2048]{1,0:T(8,128)(2,1)S(1)}, u32[]{:S(2)}, u32[]{:S(2)}) collective-permute-start(bf16[40,2048]{1,0:T(8,128)(2,1)S(1)} %pad_maximum_fusion.5.refs_0_), channel_id=1, source_target_pairs={{0,96},{16,112},{32,0},{48,16},{64,32},{80,48},{96,64},{112,80},{1... | collective-permute-start | bytes 491528 | tf_op jit(solution)/shard_map/ppermute | solution.py:23
  8.5 9.5 %collective-permute-start.3 = (bf16[40,2048]{1,0:T(8,128)(2,1)S(1)}, bf16[40,2048]{1,0:T(8,128)(2,1)S(1)}, u32[]{:S(2)}, u32[]{:S(2)}) collective-permute-start(bf16[40,2048]{1,0:T(8,128)(2,1)S(1)} %pad_maximum_fusion.5.refs_0_), channel_id=1, source_target_pairs={{0,32},{16,48},{32,64},{48,80},{64,96},{80,112},{96,0},{112,16},{1... | collective-permute-start | bytes 491528 | tf_op jit(solution)/shard_map/ppermute | solution.py:23
  8.5 11.1 %collective-permute-start = (bf16[40,2048]{1,0:T(8,128)(2,1)S(1)}, bf16[40,2048]{1,0:T(8,128)(2,1)S(1)}, u32[]{:S(2)}, u32[]{:S(2)}) collective-permute-start(bf16[40,2048]{1,0:T(8,128)(2,1)S(1)} %pad_maximum_fusion.5.refs_0_), channel_id=1, source_target_pairs={{0,112},{16,0},{32,16},{48,32},{64,48},{80,64},{96,80},{112,96},{1... | collective-permute-start | bytes 491528 | tf_op jit(solution)/shard_map/ppermute | solution.py:23
  11.7 11.6 %collective-permute-start.7 = (bf16[40,2048]{1,0:T(8,128)(2,1)S(1)}, bf16[40,2048]{1,0:T(8,128)(2,1)S(1)}, u32[]{:S(2)}, u32[]{:S(2)}) collective-permute-start(bf16[40,2048]{1,0:T(8,128)(2,1)S(1)} %pad_maximum_fusion.5.refs_0_), channel_id=1, source_target_pairs={{0,16},{16,32},{32,48},{48,64},{64,80},{80,96},{96,112},{112,0},{1... | collective-permute-start | bytes 491528 | tf_op jit(solution)/shard_map/ppermute | solution.py:23
  13.9 13.6 %collective-permute-start.2 = (bf16[40,2048]{1,0:T(8,128)(2,1)S(1)}, bf16[40,2048]{1,0:T(8,128)(2,1)S(1)}, u32[]{:S(2)}, u32[]{:S(2)}) collective-permute-start(bf16[40,2048]{1,0:T(8,128)(2,1)S(1)} %collective-permute-done.1.refs_2_), channel_id=1, source_target_pairs={{0,112},{16,0},{32,16},{48,32},{64,48},{80,64},{96,80},{112,96},{1... | collective-permute-start | bytes 491528 | tf_op jit(solution)/shard_map/ppermute | solution.py:23
  18.0 9.4 %collective-permute-start.6 = (bf16[40,2048]{1,0:T(8,128)(2,1)S(1)}, bf16[40,2048]{1,0:T(8,128)(2,1)S(1)}, u32[]{:S(2)}, u32[]{:S(2)}) collective-permute-start(bf16[40,2048]{1,0:T(8,128)(2,1)S(1)} %collective-permute-done.3.refs_7_), channel_id=1, source_target_pairs={{0,16},{16,32},{32,48},{48,64},{64,80},{80,96},{96,112},{112,0},{1... | collective-permute-start | bytes 491528 | tf_op jit(solution)/shard_map/ppermute | solution.py:23
  19.6 7.9 %collective-permute-start.4 = (bf16[40,1024]{1,0:T(8,128)(2,1)S(1)}, bf16[40,1024]{1,0:T(8,128)(2,1)S(1)}, u32[]{:S(2)}, u32[]{:S(2)}) collective-permute-start(bf16[40,1024]{1,0:T(8,128)(2,1)S(1)} %slice.48), channel_id=1, source_target_pairs={{0,32},{16,48},{32,64},{48,80},{64,96},{80,112},{96,0},{112,16},{1... | collective-permute-start | bytes 245768 | tf_op jit(solution)/shard_map/ppermute | solution.py:23
  19.6 7.9 %collective-permute-start.5 = (bf16[40,1024]{1,0:T(8,128)(2,1)S(1)}, bf16[40,1024]{1,0:T(8,128)(2,1)S(1)}, u32[]{:S(2)}, u32[]{:S(2)}) collective-permute-start(bf16[40,1024]{1,0:T(8,128)(2,1)S(1)} %slice.49), channel_id=1, source_target_pairs={{0,96},{16,112},{32,0},{48,16},{64,32},{80,48},{96,64},{112,80},{1... | collective-permute-start | bytes 245768 | tf_op jit(solution)/shard_map/ppermute | solution.py:23
  30.1 23.1 %all-to-all-start.2 = ((bf16[4,160,512]{2,1,0:T(8,128)(2,1)}), bf16[4,160,512]{2,1,0:T(8,128)(2,1)S(1)}, u32[]{:S(2)}, u32[]{:S(2)}) async-start(bf16[4,160,512]{2,1,0:T(8,128)(2,1)} %get-tuple-element.46), calls=%async_computation.2 | async-start | bytes 1310720 | tf_op jit(solution)/shard_map/all_to_all | solution.py:41
  34.3 3.1 %copy-start = (bf16[2048,1792]{1,0:T(8,128)(2,1)S(1)}, bf16[2048,1792]{1,0:T(8,128)(2,1)}, u32[]{:S(2)}) copy-start(bf16[2048,1792]{1,0:T(8,128)(2,1)} %gate.5) | copy-start | bytes 22020100
  37.4 3.1 %copy-start.3 = (bf16[2048,1792]{1,0:T(8,128)(2,1)S(1)}, bf16[2048,1792]{1,0:T(8,128)(2,1)}, u32[]{:S(2)}) copy-start(bf16[2048,1792]{1,0:T(8,128)(2,1)} %up.5) | copy-start | bytes 22020100
  40.5 3.1 %copy-start.6 = (bf16[1792,2048]{1,0:T(8,128)(2,1)S(1)}, bf16[1792,2048]{1,0:T(8,128)(2,1)}, u32[]{:S(2)}) copy-start(bf16[1792,2048]{1,0:T(8,128)(2,1)} %down.5) | copy-start | bytes 22020100
  49.6 40.7 %collective-permute-start.8 = (f32[160,2688]{1,0:T(8,128)}, f32[160,2688]{1,0:T(8,128)}, u32[]{:S(2)}, u32[]{:S(2)}) collective-permute-start(f32[160,2688]{1,0:T(8,128)} %shard_map.94), channel_id=1, source_target_pairs={{0,128},{128,0},{1,129},{129,1},{2,130},{130,2},{3,131},{131,3},{4... | collective-permute-start | bytes 5160968 | tf_op jit(solution)/shard_map/ppermute | solution.py:37
  53.2 21.8 %all-to-all-start.1 = ((bf16[4,160,1024]{2,1,0:T(8,128)(2,1)}), bf16[4,160,1024]{2,1,0:T(8,128)(2,1)S(1)}, u32[]{:S(2)}, u32[]{:S(2)}) async-start(bf16[4,160,1024]{2,1,0:T(8,128)(2,1)} %copy-done.19), calls=%async_computation.1 | async-start | bytes 2621440 | tf_op jit(solution)/shard_map/all_to_all | solution.py:41
  57.2 36.1 %collective-permute-start.22 = (bf16[4,160,512]{2,1,0:T(8,128)(2,1)S(1)}, bf16[4,160,512]{2,1,0:T(8,128)(2,1)}, u32[]{:S(2)}, u32[]{:S(2)}) collective-permute-start(bf16[4,160,512]{2,1,0:T(8,128)(2,1)S(1)} %all-to-all-done.2.refs_4_), channel_id=1, source_target_pairs={{0,128},{128,0},{1,129},{129,1},{2,130},{130,2},{3,131},{131,3},{4... | collective-permute-start | bytes 1966088 | tf_op jit(solution)/shard_map/ppermute | solution.py:37
  75.0 68.6 %collective-permute-start.14 = (bf16[4,160,1024]{2,1,0:T(8,128)(2,1)S(1)}, bf16[4,160,1024]{2,1,0:T(8,128)(2,1)}, u32[]{:S(2)}, u32[]{:S(2)}) collective-permute-start(bf16[4,160,1024]{2,1,0:T(8,128)(2,1)S(1)} %all-to-all-done.1.refs_4_), channel_id=1, source_target_pairs={{0,128},{128,0},{1,129},{129,1},{2,130},{130,2},{3,131},{131,3},{4... | collective-permute-start | bytes 3932168 | tf_op jit(solution)/shard_map/ppermute | solution.py:37
  76.1 3.1 %copy-start.1 = (bf16[2048,1792]{1,0:T(8,128)(2,1)S(1)}, bf16[2048,1792]{1,0:T(8,128)(2,1)}, u32[]{:S(2)}) copy-start(bf16[2048,1792]{1,0:T(8,128)(2,1)} %gate.5) | copy-start | bytes 22020100
  79.1 3.1 %copy-start.4 = (bf16[2048,1792]{1,0:T(8,128)(2,1)S(1)}, bf16[2048,1792]{1,0:T(8,128)(2,1)}, u32[]{:S(2)}) copy-start(bf16[2048,1792]{1,0:T(8,128)(2,1)} %up.5) | copy-start | bytes 22020100
  82.2 3.1 %copy-start.7 = (bf16[1792,2048]{1,0:T(8,128)(2,1)S(1)}, bf16[1792,2048]{1,0:T(8,128)(2,1)}, u32[]{:S(2)}) copy-start(bf16[1792,2048]{1,0:T(8,128)(2,1)} %down.5) | copy-start | bytes 22020100
  92.3 13.6 %collective-permute-start.11 = (bf16[160,1408]{1,0:T(8,128)(2,1)S(1)}, bf16[160,1408]{1,0:T(8,128)(2,1)S(1)}, u32[]{:S(2)}, u32[]{:S(2)}) collective-permute-start(bf16[160,1408]{1,0:T(8,128)(2,1)S(1)} %get-tuple-element.33.a_own.refs_0_), channel_id=1, source_target_pairs={{0,1},{1,2},{2,3},{3,0},{4,5},{5,6},{6,7},{7,4},{8,9},{9,10},{10,1... | collective-permute-start | bytes 1351688 | tf_op jit(solution)/shard_map/ppermute | solution.py:28
  92.8 16.0 %collective-permute-start.9 = (bf16[160,1408]{1,0:T(8,128)(2,1)S(1)}, bf16[160,1408]{1,0:T(8,128)(2,1)S(1)}, u32[]{:S(2)}, u32[]{:S(2)}) collective-permute-start(bf16[160,1408]{1,0:T(8,128)(2,1)S(1)} %get-tuple-element.33.a_own.refs_0_), channel_id=1, source_target_pairs={{0,128},{128,0},{1,129},{129,1},{2,130},{130,2},{3,131},{131,3},{4... | collective-permute-start | bytes 1351688 | tf_op jit(solution)/shard_map/ppermute | solution.py:37
  93.1 2.1 %collective-permute-start.10 = (bf16[160,1280]{1,0:T(8,128)(2,1)S(1)}, bf16[160,1280]{1,0:T(8,128)(2,1)S(1)}, u32[]{:S(2)}, u32[]{:S(2)}) collective-permute-start(bf16[160,1280]{1,0:T(8,128)(2,1)S(1)} %get-tuple-element.34.b_own.refs_0_), channel_id=1, source_target_pairs={{0,128},{128,0},{1,129},{129,1},{2,130},{130,2},{3,131},{131,3},{4... | collective-permute-start | bytes 1228808 | tf_op jit(solution)/shard_map/ppermute | solution.py:37
  93.3 12.7 %collective-permute-start.19 = (bf16[160,1280]{1,0:T(8,128)(2,1)S(1)}, bf16[160,1280]{1,0:T(8,128)(2,1)}, u32[]{:S(2)}, u32[]{:S(2)}) collective-permute-start(bf16[160,1280]{1,0:T(8,128)(2,1)S(1)} %get-tuple-element.34.b_own.refs_0_), channel_id=1, source_target_pairs={{0,4},{1,5},{2,6},{3,7},{4,8},{5,9},{6,10},{7,11},{8,12},{9,13},{1... | collective-permute-start | bytes 1228808 | tf_op jit(solution)/shard_map/ppermute | solution.py:33
  95.9 47.6 %collective-permute-start.12 = (bf16[160,1408]{1,0:T(8,128)(2,1)S(1)}, bf16[160,1408]{1,0:T(8,128)(2,1)}, u32[]{:S(2)}, u32[]{:S(2)}) collective-permute-start(bf16[160,1408]{1,0:T(8,128)(2,1)S(1)} %get-tuple-element.33.a_own.refs_0_), channel_id=1, source_target_pairs={{0,3},{1,0},{2,1},{3,2},{4,7},{5,4},{6,5},{7,6},{8,11},{9,8},{10,9... | collective-permute-start | bytes 1351688 | tf_op jit(solution)/shard_map/ppermute | solution.py:28
  105.8 25.7 %copy-start.20 = (bf16[160,1408]{1,0:T(8,128)(2,1)}, bf16[160,1408]{1,0:T(8,128)(2,1)S(1)}, u32[]{:S(2)}) copy-start(bf16[160,1408]{1,0:T(8,128)(2,1)S(1)} %collective-permute-done.11.refs_1_) | copy-start | bytes 1351684
  105.8 37.8 %collective-permute-start.13 = (bf16[160,1408]{1,0:T(8,128)(2,1)S(1)}, bf16[160,1408]{1,0:T(8,128)(2,1)}, u32[]{:S(2)}, u32[]{:S(2)}) collective-permute-start(bf16[160,1408]{1,0:T(8,128)(2,1)S(1)} %collective-permute-done.11.refs_1_), channel_id=1, source_target_pairs={{0,1},{1,2},{2,3},{3,0},{4,5},{5,6},{6,7},{7,4},{8,9},{9,10},{10,1... | collective-permute-start | bytes 1351688 | tf_op jit(solution)/shard_map/ppermute | solution.py:28
  106.0 25.5 %collective-permute-start.20 = (bf16[160,1280]{1,0:T(8,128)(2,1)S(1)}, bf16[160,1280]{1,0:T(8,128)(2,1)}, u32[]{:S(2)}, u32[]{:S(2)}) collective-permute-start(bf16[160,1280]{1,0:T(8,128)(2,1)S(1)} %get-tuple-element.34.b_own.refs_0_), channel_id=1, source_target_pairs={{0,12},{1,13},{2,14},{3,15},{4,0},{5,1},{6,2},{7,3},{8,4},{9,5},{1... | collective-permute-start | bytes 1228808 | tf_op jit(solution)/shard_map/ppermute | solution.py:33
  109.5 22.0 %collective-permute-start.21 = (bf16[160,1280]{1,0:T(8,128)(2,1)}, bf16[160,1280]{1,0:T(8,128)(2,1)}, u32[]{:S(2)}, u32[]{:S(2)}) collective-permute-start(bf16[160,1280]{1,0:T(8,128)(2,1)} %collective-permute-done.19.refs_1_), channel_id=1, source_target_pairs={{0,4},{1,5},{2,6},{3,7},{4,8},{5,9},{6,10},{7,11},{8,12},{9,13},{1... | collective-permute-start | bytes 1228808 | tf_op jit(solution)/shard_map/ppermute | solution.py:33
  109.8 3.1 %copy-start.2 = (bf16[2048,1792]{1,0:T(8,128)(2,1)S(1)}, bf16[2048,1792]{1,0:T(8,128)(2,1)}, u32[]{:S(2)}) copy-start(bf16[2048,1792]{1,0:T(8,128)(2,1)} %gate.5) | copy-start | bytes 22020100
  112.8 3.1 %copy-start.5 = (bf16[2048,1792]{1,0:T(8,128)(2,1)S(1)}, bf16[2048,1792]{1,0:T(8,128)(2,1)}, u32[]{:S(2)}) copy-start(bf16[2048,1792]{1,0:T(8,128)(2,1)} %up.5) | copy-start | bytes 22020100
  115.9 3.1 %copy-start.8 = (bf16[1792,2048]{1,0:T(8,128)(2,1)S(1)}, bf16[1792,2048]{1,0:T(8,128)(2,1)}, u32[]{:S(2)}) copy-start(bf16[1792,2048]{1,0:T(8,128)(2,1)} %down.5) | copy-start | bytes 22020100
  131.5 12.1 %copy-start.21 = (bf16[160,1408]{1,0:T(8,128)(2,1)S(1)}, bf16[160,1408]{1,0:T(8,128)(2,1)}, u32[]{:S(2)}) copy-start(bf16[160,1408]{1,0:T(8,128)(2,1)} %copy-done.20) | copy-start | bytes 1351684
  140.9 25.5 %collective-permute-start.23 = (bf16[128,1280]{1,0:T(8,128)(2,1)}, bf16[128,1280]{1,0:T(8,128)(2,1)S(1)}, u32[]{:S(2)}, u32[]{:S(2)}) collective-permute-start(bf16[128,1280]{1,0:T(8,128)(2,1)} %get-tuple-element.50), channel_id=1, source_target_pairs={{0,1},{1,2},{2,3},{3,0},{4,5},{5,6},{6,7},{7,4},{8,9},{9,10},{10,1... | collective-permute-start | bytes 983048 | tf_op jit(solution)/shard_map/ppermute | solution.py:28
  140.9 25.5 %collective-permute-start.24 = (bf16[128,1280]{1,0:T(8,128)(2,1)}, bf16[128,1280]{1,0:T(8,128)(2,1)}, u32[]{:S(2)}, u32[]{:S(2)}) collective-permute-start(bf16[128,1280]{1,0:T(8,128)(2,1)} %get-tuple-element.51), channel_id=1, source_target_pairs={{0,3},{1,0},{2,1},{3,2},{4,7},{5,4},{6,5},{7,6},{8,11},{9,8},{10,9... | collective-permute-start | bytes 983048 | tf_op jit(solution)/shard_map/ppermute | solution.py:28
  152.4 9.8 %collective-permute-start.15 = (bf16[128,1408]{1,0:T(8,128)(2,1)}, bf16[128,1408]{1,0:T(8,128)(2,1)}, u32[]{:S(2)}, u32[]{:S(2)}) collective-permute-start(bf16[128,1408]{1,0:T(8,128)(2,1)} %get-tuple-element.41), channel_id=1, source_target_pairs={{0,4},{1,5},{2,6},{3,7},{4,8},{5,9},{6,10},{7,11},{8,12},{9,13},{1... | collective-permute-start | bytes 1081352 | tf_op jit(solution)/shard_map/ppermute | solution.py:33
  152.6 9.6 %collective-permute-start.16 = (bf16[128,1408]{1,0:T(8,128)(2,1)}, bf16[128,1408]{1,0:T(8,128)(2,1)}, u32[]{:S(2)}, u32[]{:S(2)}) collective-permute-start(bf16[128,1408]{1,0:T(8,128)(2,1)} %get-tuple-element.42), channel_id=1, source_target_pairs={{0,12},{1,13},{2,14},{3,15},{4,0},{5,1},{6,2},{7,3},{8,4},{9,5},{1... | collective-permute-start | bytes 1081352 | tf_op jit(solution)/shard_map/ppermute | solution.py:33
  156.4 5.8 %copy-start.10 = (f32[256,1408]{1,0:T(8,128)S(1)}, f32[256,1408]{1,0:T(8,128)}, u32[]{:S(2)}) copy-start(f32[256,1408]{1,0:T(8,128)} %copy-done.9) | copy-start | bytes 4325380
  156.4 42.6 %all-to-all-start = ((bf16[8,20,4096]{2,1,0:T(8,128)(2,1)}), bf16[8,20,4096]{2,1,0:T(8,128)(2,1)}, u32[]{:S(2)}, u32[]{:S(2)}) async-start(bf16[8,20,4096]{2,1,0:T(8,128)(2,1)} %pad_maximum_fusion), calls=%async_computation | async-start | bytes 3145728 | tf_op jit(solution)/shard_map/all_to_all | solution.py:347
  162.2 4.2 %copy-start.14 = (f32[256,1280]{1,0:T(8,128)S(1)}, f32[256,1280]{1,0:T(8,128)}, u32[]{:S(2)}) copy-start(f32[256,1280]{1,0:T(8,128)} %copy-done.13) | copy-start | bytes 3932164
  162.2 4.2 %copy-start.16 = (f32[256,1280]{1,0:T(8,128)S(1)}, f32[256,1280]{1,0:T(8,128)}, u32[]{:S(2)}) copy-start(f32[256,1280]{1,0:T(8,128)} %copy-done.15) | copy-start | bytes 3932164
  163.7 16.4 %collective-permute-start.17 = (bf16[256,1408]{1,0:T(8,128)(2,1)S(1)}, bf16[256,1408]{1,0:T(8,128)(2,1)S(1)}, u32[]{:S(2)}, u32[]{:S(2)}) collective-permute-start(bf16[256,1408]{1,0:T(8,128)(2,1)S(1)} %get-tuple-element.43), channel_id=1, source_target_pairs={{0,4},{1,5},{2,6},{3,7},{4,8},{5,9},{6,10},{7,11},{8,12},{9,13},{1... | collective-permute-start | bytes 2162696 | tf_op jit(solution)/shard_map/ppermute | solution.py:33
  164.3 15.7 %collective-permute-start.18 = (bf16[256,1408]{1,0:T(8,128)(2,1)S(1)}, bf16[256,1408]{1,0:T(8,128)(2,1)S(1)}, u32[]{:S(2)}, u32[]{:S(2)}) collective-permute-start(bf16[256,1408]{1,0:T(8,128)(2,1)S(1)} %get-tuple-element.44), channel_id=1, source_target_pairs={{0,12},{1,13},{2,14},{3,15},{4,0},{5,1},{6,2},{7,3},{8,4},{9,5},{1... | collective-permute-start | bytes 2162696 | tf_op jit(solution)/shard_map/ppermute | solution.py:33
  166.4 13.6 %copy-start.12 = (f32[256,1408]{1,0:T(8,128)S(1)}, f32[256,1408]{1,0:T(8,128)}, u32[]{:S(2)}) copy-start(f32[256,1408]{1,0:T(8,128)} %copy-done.11) | copy-start | bytes 4325380
  167.7 16.1 %copy-start.18 = (f32[256,1280]{1,0:T(8,128)S(1)}, f32[256,1280]{1,0:T(8,128)}, u32[]{:S(2)}) copy-start(f32[256,1280]{1,0:T(8,128)} %copy-done.17) | copy-start | bytes 3932164
  167.7 16.1 %collective-permute-start.25 = (bf16[256,1280]{1,0:T(8,128)(2,1)S(1)}, bf16[256,1280]{1,0:T(8,128)(2,1)S(1)}, u32[]{:S(2)}, u32[]{:S(2)}) collective-permute-start(bf16[256,1280]{1,0:T(8,128)(2,1)S(1)} %get-tuple-element.52), channel_id=1, source_target_pairs={{0,1},{1,2},{2,3},{3,0},{4,5},{5,6},{6,7},{7,4},{8,9},{9,10},{10,1... | collective-permute-start | bytes 1966088 | tf_op jit(solution)/shard_map/ppermute | solution.py:28
  167.8 16.0 %collective-permute-start.26 = (bf16[256,1280]{1,0:T(8,128)(2,1)S(1)}, bf16[256,1280]{1,0:T(8,128)(2,1)S(1)}, u32[]{:S(2)}, u32[]{:S(2)}) collective-permute-start(bf16[256,1280]{1,0:T(8,128)(2,1)S(1)} %get-tuple-element.53), channel_id=1, source_target_pairs={{0,3},{1,0},{2,1},{3,2},{4,7},{5,4},{6,5},{7,6},{8,11},{9,8},{10,9... | collective-permute-start | bytes 1966088 | tf_op jit(solution)/shard_map/ppermute | solution.py:28
  180.3 7.5 %collective-permute-start.27 = (bf16[128,1408]{1,0:T(8,128)(2,1)S(1)}, bf16[128,1408]{1,0:T(8,128)(2,1)S(1)}, u32[]{:S(2)}, u32[]{:S(2)}) collective-permute-start(bf16[128,1408]{1,0:T(8,128)(2,1)S(1)} %get-tuple-element.55), channel_id=1, source_target_pairs={{0,128},{128,0},{1,129},{129,1},{2,130},{130,2},{3,131},{131,3},{4... | collective-permute-start | bytes 1081352 | tf_op jit(solution)/shard_map/ppermute | solution.py:37
  184.0 3.7 %collective-permute-start.28 = (bf16[128,1280]{1,0:T(8,128)(2,1)S(1)}, bf16[128,1280]{1,0:T(8,128)(2,1)S(1)}, u32[]{:S(2)}, u32[]{:S(2)}) collective-permute-start(bf16[128,1280]{1,0:T(8,128)(2,1)S(1)} %get-tuple-element.56), channel_id=1, source_target_pairs={{0,128},{128,0},{1,129},{129,1},{2,130},{130,2},{3,131},{131,3},{4... | collective-permute-start | bytes 983048 | tf_op jit(solution)/shard_map/ppermute | solution.py:37
  (10 other events, 10.2 us)
where the time goes:
time: 202 us; the launch traced here: 201 us
  starting transfers between devices  61.7 us (31%)
  waiting for transfers between devices  52.4 us (26%)
  Pallas kernels  40.7 us (20%)
  local copies, waits for them, and re-layouts  39.7 us (20%)
  other arithmetic  6.05 us (3%)
    unnamed x53, local copies, waits for them, and re-layouts  38.9 us
    ppermute x8, starting transfers between devices, to_z(): lax.ppermute(value, 'col', [(k, (k + step) % COLS) for k in range(COLS)])  19.3 us
    all_to_all x2, waiting for transfers between devices, swap(): lax.all_to_all(value, 'depth', split_axis=0, concat_axis=0, axis_index_gr...  17.5 us
    pallas_call x2, Pallas kernels, weight_partials(): pl.pallas_call(functools.partial(weight_kernel, cut), in_specs=[pl.BlockS...  12.6 us
    ppermute x7, starting transfers between devices, to_core(): return lax.ppermute(value, 'row', [(0, 1), (1, 0)])  11.4 us
    ppermute x7, waiting for transfers between devices, to_y(): lax.ppermute(value, 'depth', [(k, (k + SIDE * step) % side) for k in rang...  11.1 us
    pallas_call x2, Pallas kernels, project(): pl.pallas_call(project_kernel, grid_spec=pltpu.PrefetchScalarGridSpec(num...  11.1 us
    pallas_call x1, Pallas kernels, back(): pl.pallas_call(back_kernel, grid_spec=pltpu.PrefetchScalarGridSpec(num_sc...  10.4 us
  transfers between devices with their start and end apart: 32, of which 10 were waited for; matrix products, arithmetic and copies ran while one was open for 2% of the time, Pallas kernels for 19%

commit v1 on v0

--- a/solution.py
+++ b/solution.py
@@ -47,7 +47,15 @@
     return jax.ShapeDtypeStruct(dims, dtype)
 
 
-def call(kernel, outs, *args, limit=32, scratch=()):
+def hbm(*values):
+    return [pltpu.with_memory_space_constraint(value, pltpu.HBM) for value in values]
+
+
+def cost(flops, moved):
+    return pl.CostEstimate(flops=flops, bytes_accessed=moved, transcendentals=0)
+
+
+def call(kernel, outs, *args, limit=16, scratch=()):
     return pl.pallas_call(
         kernel,
         out_shape=outs,
@@ -91,6 +99,10 @@
     return [value, after, after2, after3, *far, before3, before2, before]
 
 
+def chunks(extent, size=256):
+    return [(start, min(size, extent - start)) for start in range(0, extent, size)]
+
+
 def project_kernel(which, feat, upst, gate, up, down, out):
     width = gate.shape[1]
     products = (
@@ -110,9 +122,9 @@
             out[place] = out[place] + product
 
 
-def project(which, features, upstream, gate_weight, up_weight, down_weight):
+def project(which, features, upstream, weights):
     group, model = features.shape
-    half = gate_weight.shape[1] // 2
+    half = weights[0].shape[1] // 2
     step = model // 4
     return pl.pallas_call(
         project_kernel,
@@ -129,8 +141,9 @@
             out_specs=pl.BlockSpec((group, 3 * half), lambda k, w: (0, 0)),
         ),
         out_shape=shape(group, 3 * half, dtype=F32),
-        compiler_params=pltpu.CompilerParams(vmem_limit_bytes=24 * MIB),
-    )(which, features, upstream, gate_weight, up_weight, down_weight)
+        cost_estimate=cost(6 * group * model * half, 6 * model * half),
+        compiler_params=pltpu.CompilerParams(vmem_limit_bytes=20 * MIB),
+    )(which, features, upstream, *hbm(*weights))
 
 
 def swiglu_kernel(own, theirs, route_a, route_b):
@@ -149,7 +162,7 @@
     route_b[:, half - cut :] = (hidden_grad * gate_pre * logistic).astype(BF)
 
 
-def back_kernel(place, a_own, b_own, a_theirs, b_theirs, down, gate, up, out, inp, total):
+def back_kernel(place, a_own, b_own, a_theirs, b_theirs, gate, up, down, out, inp, total):
     half = down.shape[0]
     cut = a_own.shape[1] - half
     rest = half - cut
@@ -157,8 +170,8 @@
     inner = pl.program_id(1)
 
     def add(a, b):
+        first = dot(a[:, :half], down[...], ((1,), (0,)))
         grads = jnp.concatenate([a[:, half:], b[:, :rest]], axis=1)
-        first = dot(a[:, :half], down[...], ((1,), (0,)))
         second = dot(grads, gate[...], ((1,), (1,))) + dot(b[:, rest:], up[...], ((1,), (1,)))
         return first, second
 
@@ -173,12 +186,13 @@
         second = total[1] + second
         for k in range(COLS):
             at = lax.rem(place[1] + k, COLS)
-            out[at] = first[rows * k : rows * (k + 1)].astype(BF)
-            inp[at] = second[rows * k : rows * (k + 1)].astype(BF)
-
-
-def back(place, routes, down_weight, gate_weight, up_weight, rows):
-    units, model = down_weight.shape
+            block = slice(rows * k, rows * (k + 1))
+            out[at] = first[block].astype(BF)
+            inp[at] = second[block].astype(BF)
+
+
+def back(place, routes, weights, rows):
+    model, units = weights[0].shape
     half = units // 2
     step = model // 4
 
@@ -196,51 +210,76 @@
             grid=(model // step, 2),
             in_specs=[whole(r) for r in routes]
             + [
-                pl.BlockSpec((half, step), lambda n, j, p: (pick(j, p), n)),
                 pl.BlockSpec((step, half), lambda n, j, p: (n, pick(j, p))),
                 pl.BlockSpec((step, half), lambda n, j, p: (n, pick(j, p))),
+                pl.BlockSpec((half, step), lambda n, j, p: (pick(j, p), n)),
             ],
             out_specs=[block, block],
             scratch_shapes=[pltpu.VMEM((2, COLS * rows, step), F32)],
         ),
         out_shape=[shape(COLS, rows, model)] * 2,
-        compiler_params=pltpu.CompilerParams(vmem_limit_bytes=24 * MIB),
-    )(place, *routes, down_weight, gate_weight, up_weight)
-
-
-def weight_kernel(cut, place, *refs):
+        cost_estimate=cost(6 * COLS * rows * model * units, 6 * model * units),
+        compiler_params=pltpu.CompilerParams(vmem_limit_bytes=20 * MIB),
+    )(place, *hbm(*routes, *weights))
+
+
+def weight_kernel(cut, far, place, *refs):
     pieces, columns = refs[:4], refs[4:6]
-    own, before, after, far_a, far_b, total = refs[6:]
+    outs, (piece, rows, sems) = refs[6:-3], refs[-3:]
+    group, wide = pieces[0].shape
     width = SIDE * LANES
-    for t in range(2):
-        for s, (piece, offset) in enumerate(zip(pieces, (0, SIDE - 1, 1, 2))):
-            rows = columns[t][lax.rem(place[0] + offset, SIDE)]
-            part = dot(rows[:, :width], piece[:, cut:], ((0,), (0,)))
-            total[:, cut:] = part if s == 0 else total[:, cut:] + part
-            if cut:
-                part = dot(rows[:, width:], piece[:, :cut], ((0,), (0,)))
-                total[:, :cut] = part if s == 0 else total[:, :cut] + part
-        here = pl.ds(LANES * t, LANES)
-        for ref, offset in ((own, 0), (before, SIDE - 1), (after, 1), ((far_a, far_b)[t], 2)):
-            start = pl.multiple_of(LANES * lax.rem(place[1] + offset, SIDE), LANES)
-            value = total[pl.ds(start, LANES), :]
-            if ref is far_a or ref is far_b:
-                ref[...] = value.astype(BF)
+    offsets = (2,) if far else (SIDE - 1, 1, 0)
+    bases = (0, width) if cut else (0,)
+    starts = [lax.rem(place[1] + offset, SIDE) for offset in offsets]
+    copies = []
+    for s, offset in enumerate((0, SIDE - 1, 1, 2)):
+        here = pl.ds(group * s, group)
+        source = lax.rem(place[0] + offset, SIDE)
+        moves = [(pieces[s], piece.at[here])]
+        for t in range(2):
+            for i, start in enumerate(starts):
+                for j, base in enumerate(bases):
+                    at = pl.ds(pl.multiple_of(base + LANES * start, LANES), LANES)
+                    to = pl.ds(LANES * (2 * (i * len(bases) + j) + t), LANES)
+                    moves.append((columns[t].at[source, :, at], rows.at[here, to]))
+        for k, (left, right) in enumerate(moves):
+            copies.append(pltpu.make_async_copy(left, right, sems.at[s, k]))
+    for copy in copies:
+        copy.start()
+    for copy in copies:
+        copy.wait()
+    for i in range(len(offsets)):
+        for j, (first, last) in enumerate(((cut, wide), (0, cut))[: len(bases)]):
+            column = 2 * LANES * (i * len(bases) + j)
+            left = rows[:, column : column + 2 * LANES]
+            value = dot(left, piece[:, first:last], ((0,), (0,)))
+            if far:
+                outs[0][:, first:last] = value[:LANES].astype(BF)
+                outs[1][:, first:last] = value[LANES:].astype(BF)
             else:
-                ref[here, :] = value
-
-
-def weight_partials(cut, place, pieces, columns):
-    wide = pieces[0].shape[1]
-    vmem = pl.BlockSpec(memory_space=pltpu.VMEM)
+                outs[i][:, first:last] = value
+
+
+def weight_partials(cut, far, place, pieces, columns):
+    group, wide = pieces[0].shape
+    count = (1 if far else 3) * (2 if cut else 1)
+    outs = [shape(LANES, wide)] * 2 if far else [shape(2 * LANES, wide, dtype=F32)] * 3
     return pl.pallas_call(
-        functools.partial(weight_kernel, cut),
-        in_specs=[pl.BlockSpec(memory_space=pltpu.SMEM)] + [vmem] * 6,
-        out_specs=[vmem] * 5,
-        out_shape=[shape(2 * LANES, wide, dtype=F32)] * 3 + [shape(LANES, wide)] * 2,
-        scratch_shapes=[pltpu.VMEM((SIDE * LANES, wide), F32)],
-        compiler_params=pltpu.CompilerParams(vmem_limit_bytes=32 * MIB),
-    )(place, *pieces, *columns)
+        functools.partial(weight_kernel, cut, far),
+        in_specs=[pl.BlockSpec(memory_space=pltpu.SMEM)]
+        + [pl.BlockSpec(memory_space=pl.ANY)] * 6,
+        out_specs=[pl.BlockSpec(memory_space=pltpu.VMEM)] * len(outs),
+        out_shape=outs,
+        scratch_shapes=[
+            pltpu.VMEM((SIDE * group, wide), BF),
+            pltpu.VMEM((SIDE * group, 2 * LANES * count), BF),
+            pltpu.SemaphoreType.DMA((SIDE, 1 + 2 * count)),
+        ],
+        cost_estimate=cost(
+            16 * group * LANES * wide * len(outs), 2 * SIDE * group * (wide + 2 * LANES * count)
+        ),
+        compiler_params=pltpu.CompilerParams(vmem_limit_bytes=20 * MIB),
+    )(place, *hbm(*pieces, *columns))
 
 
 def pass_on_kernel(before, after, from_before, from_after, send_before, send_after):
@@ -257,10 +296,11 @@
     theirs[...] = total[LANES:].astype(BF)
 
 
-def scatter(parts, send):
-    own, before, after, far_a, far_b = parts
-    wide = own.shape[1]
+def scatter(cut, place, pieces, columns, send):
+    wide = pieces[0].shape[1]
+    far_a, far_b = weight_partials(cut, True, place, pieces, columns)
     from_before, from_after = send(far_a, 1), send(far_b, -1)
+    before, after, own = weight_partials(cut, False, place, pieces, columns)
     pair = [shape(2 * LANES, wide)] * 2
     send_before, send_after = call(pass_on_kernel, pair, before, after, from_before, from_after)
     from_before, from_after = send(send_after, 1), send(send_before, -1)
@@ -268,6 +308,52 @@
     return call(sum_kernel, pair, own, from_before, from_after)
 
 
+def finish_kernel(which, mine_a, other_a, mine_b, other_b, gate, up, down):
+    half = gate.shape[1] // 2
+    cut = mine_a.shape[1] - half
+    rest = half - cut
+
+    def place(a, b, base):
+        gate[:, base : base + cut] = a[:, half:]
+        gate[:, base + cut : base + half] = b[:, :rest]
+        up[:, base : base + half] = b[:, rest:]
+        down[base : base + half, :] = a[:, :half].T
+
+    @pl.when(which[0] == 0)
+    def _():
+        place(mine_a, mine_b, 0)
+        place(other_a, other_b, half)
+
+    @pl.when(which[0] != 0)
+    def _():
+        place(other_a, other_b, 0)
+        place(mine_a, mine_b, half)
+
+
+def total_kernel(moved, out, grad):
+    model = out.shape[1]
+    total = moved[0].astype(F32)
+    for k in range(1, COLS):
+        total = total + moved[k].astype(F32)
+    out[...] = total[:, :model].astype(BF)
+    grad[...] = total[:, model:].astype(BF)
+
+
+def gather(value, send):
+    before, after = send(value, 1), send(value, -1)
+    return [value, before, after, send(after, -1)]
+
+
+def call_at(kernel, outs, which, *args):
+    return pl.pallas_call(
+        kernel,
+        in_specs=[pl.BlockSpec(memory_space=pltpu.SMEM)]
+        + [pl.BlockSpec(memory_space=pltpu.VMEM)] * len(args),
+        out_shape=outs,
+        compiler_params=pltpu.CompilerParams(vmem_limit_bytes=16 * MIB),
+    )(which, *args)
+
+
 def gather(value, send):
     before, after = send(value, 1), send(value, -1)
     return [value, before, after, send(before, 1)]
@@ -275,7 +361,6 @@
 
 def body(tokens, gate_weight, up_weight, down_weight, cotangent):
     row, col, depth = (lax.axis_index(name) for name in ("row", "col", "depth"))
-    first = row == 0
     at_x, at_y = depth % SIDE, depth // SIDE
     rows, model = tokens.shape
     group = rows * COLS
@@ -289,64 +374,54 @@
         [
             shape(group, model),
             shape(group, model),
-            shape(SIDE, group, 2 * width),
-            shape(SIDE, group, width),
+            pltpu.HBM((SIDE, group, 2 * width), BF),
+            pltpu.HBM((SIDE, group, width), BF),
         ],
         *blocks,
         scratch=[pltpu.VMEM((group, model), F32)] * 2,
     )
     weights = (gate_weight, up_weight, down_weight)
-    sent = project(jnp.reshape(1 - row, (1,)), features, upstream, *weights)
-    kept = project(jnp.reshape(row, (1,)), features, upstream, *weights)
+    sent = project(jnp.reshape(1 - row, (1,)), features, upstream, weights)
+    kept = project(jnp.reshape(row, (1,)), features, upstream, weights)
     routes = call(
         swiglu_kernel,
-        [shape(group, half + cut), shape(group, 2 * half - cut)],
+        [pltpu.HBM((group, half + cut), BF), pltpu.HBM((group, 2 * half - cut), BF)],
         kept,
-        to_core(sent),
+        *hbm(to_core(sent)),
     )
     route_a, route_b = routes
-
+    wide_a = gather(route_a, to_x)
+    wide_b = gather(route_b, to_y)
+
+    send_a, _ = lax.optimization_barrier((send_a, sent))
     columns_a = swap(send_a, ALONG_X)
+    send_b, _ = lax.optimization_barrier((send_b, wide_a[1]))
     columns_b = swap(send_b, ALONG_Y)
     columns_a = (columns_a, to_core(columns_a))
     columns_b = (columns_b, to_core(columns_b))
 
-    wide_a = gather(route_a, to_x)
-    wide_b = gather(route_b, to_y)
-
     theirs = (to_core(route_a), to_core(route_b))
-    out_part, in_part = back(
-        jnp.stack([row, col]),
-        (route_a, route_b, *theirs),
-        down_weight,
-        gate_weight,
-        up_weight,
-        rows,
-    )
-
-    part_a = weight_partials(half, jnp.stack([at_x, at_y]), wide_a, columns_a)
-    part_b = weight_partials(0, jnp.stack([at_y, at_x]), wide_b, columns_b)
-    mine_a, other_a = scatter(part_a, to_y)
-    mine_b, other_b = scatter(part_b, to_x)
-    other_a, other_b = to_core(other_a), to_core(other_b)
-    rest = half - cut
-
-    def both(own, theirs):
-        return jnp.concatenate(
-            [jnp.where(first, own, theirs), jnp.where(first, theirs, own)], axis=1
-        )
-
-    def gate_of(a, b):
-        return jnp.concatenate([a[:, half:], b[:, :rest]], axis=1)
-
-    gate_grad_w = both(gate_of(mine_a, mine_b), gate_of(other_a, other_b))
-    up_grad_w = both(mine_b[:, rest:], other_b[:, rest:])
-    down_grad_w = both(mine_a[:, :half], other_a[:, :half]).T
-
-    part = jnp.concatenate([out_part, in_part], axis=2)
+    routes, _ = lax.optimization_barrier(
+        ((route_a, route_b, *theirs), (*wide_a[1:3], *wide_b[1:3]))
+    )
+    part = back(jnp.stack([row, col]), routes, weights, rows)
+    wide_a[1], wide_b[1], part = lax.optimization_barrier((wide_a[1], wide_b[1], part))
+    part = jnp.concatenate(part, axis=2)
     moved = lax.all_to_all(part, "col", split_axis=0, concat_axis=0, tiled=True)
-    total = jnp.sum(moved.astype(F32), axis=0).astype(BF)
-    return (total[:, :model], total[:, model:], gate_grad_w, up_grad_w, down_grad_w)
+    layer_out, input_grad = call(total_kernel, [shape(rows, model)] * 2, moved)
+
+    mine_a, other_a = scatter(half, jnp.stack([at_x, at_y]), wide_a, columns_a, to_y)
+    mine_b, other_b = scatter(0, jnp.stack([at_y, at_x]), wide_b, columns_b, to_x)
+    weight_grads = call_at(
+        finish_kernel,
+        [shape(LANES, 2 * half)] * 2 + [shape(2 * half, LANES)],
+        jnp.reshape(row, (1,)),
+        mine_a,
+        to_core(other_a),
+        mine_b,
+        to_core(other_b),
+    )
+    return (layer_out, input_grad, *weight_grads)
 
 
 def solution(mesh):

time: 202 us -> 163 us (0.81)
  local copies, waits for them, and re-layouts: 39.7 us -> 0.95 us
  Pallas kernels: 40.7 us -> 50.6 us
  waiting for transfers between devices: 52.4 us -> 43 us
  other arithmetic: 6.05 us -> 2.52 us
  starting transfers between devices: 61.7 us -> 64.2 us
    unnamed x53 -> x12, local copies, waits for them, and re-layouts: 38.9 us -> 0.94 us
    all_to_all x2, waiting for transfers between devices: 17.5 us -> 0.01 us  [swap(): lax.all_to_all(value, 'depth', split_axis=0, concat_axis=0, axis_index_gr...]
    ppermute x7, waiting for transfers between devices: 11.1 us -> 23 us  [to_y(): lax.ppermute(value, 'depth', [(k, (k + SIDE * step) % side) for k in rang...]
    all_to_all x1, waiting for transfers between devices: 8.44 us -> 0.01 us  [body(): moved = lax.all_to_all(part, 'col', split_axis=0, concat_axis=0, tiled=True)]
    ppermute x7, waiting for transfers between devices: 7.49 us -> 12.9 us  [to_x(): return lax.ppermute(value, 'depth', pairs)]
    pallas_call x2 -> x5, Pallas kernels: 12.6 us -> 16.5 us  [the longest x4 15.2 us: weight_partials(): pl.pallas_call(functools.partial(weight_kernel, cut, far), in_specs=[pl.B...]
    pallas_call x1, Pallas kernels: 10.4 us -> 13.7 us  [back(): pl.pallas_call(back_kernel, grid_spec=pltpu.PrefetchScalarGridSpec(num_sc...]
    ppermute x7, starting transfers between devices: 11.4 us -> 13.9 us  [to_core(): return lax.ppermute(value, 'row', [(0, 1), (1, 0)])]
  transfers between devices with their start and end apart: 32 -> 32, of which waited for: 10 -> 8; matrix products, arithmetic and copies ran while one was open for 2% -> 1% of each run, Pallas kernels for 19% -> 25%
where the time goes in v1:
time: 163 us; the launch traced here: 162 us
  starting transfers between devices  64.2 us (39%)
  Pallas kernels  50.6 us (31%)
  waiting for transfers between devices  43 us (26%)
  other arithmetic  2.52 us (2%)
    ppermute x7, waiting for transfers between devices, to_y(): lax.ppermute(value, 'depth', [(k, (k + SIDE * step) % side) for k in rang...  23 us
    ppermute x8, starting transfers between devices, to_z(): lax.ppermute(value, 'col', [(k, (k + step) % COLS) for k in range(COLS)])  19.3 us
    pallas_call x4, Pallas kernels, weight_partials(): pl.pallas_call(functools.partial(weight_kernel, cut, far), in_specs=[pl.B...  15.2 us
    ppermute x7, starting transfers between devices, to_core(): return lax.ppermute(value, 'row', [(0, 1), (1, 0)])  13.9 us
    pallas_call x1, Pallas kernels, back(): pl.pallas_call(back_kernel, grid_spec=pltpu.PrefetchScalarGridSpec(num_sc...  13.7 us
    pallas_call x2, Pallas kernels, project(): pl.pallas_call(project_kernel, grid_spec=pltpu.PrefetchScalarGridSpec(num...  13.4 us
    ppermute x7, waiting for transfers between devices, to_x(): return lax.ppermute(value, 'depth', pairs)  12.9 us
    ppermute x7, starting transfers between devices, to_y(): lax.ppermute(value, 'depth', [(k, (k + SIDE * step) % side) for k in rang...  10.3 us
  transfers between devices with their start and end apart: 32, of which 8 were waited for; matrix products, arithmetic and copies ran while one was open for 1% of the time, Pallas kernels for 25%

profile of v1, /device:TPU:1, one launch (start us, length us, event | category | flops | bytes accessed | tf_op | source)
XLA Modules:
  0.0 162.1 jit_solution(10545436651304316239)
XLA Ops:
  0.6 1.0 pad_maximum_fusion.1.refs_0_
  1.6 6.9 %collective-permute-start.1 = (bf16[40,2048]{1,0:T(8,128)(2,1)S(1)}, bf16[40,2048]{1,0:T(8,128)(2,1)S(1)}, u32[]{:S(2)}, u32[]{:S(2)}) collective-permute-start(bf16[40,2048]{1,0:T(8,128)(2,1)S(1)} %pad_maximum_fusion.1.refs_0_), channel_id=1, source_target_pairs={{0,96},{16,112},{32,0},{48,16},{64,32},{80,48},{96,64},{112,80},{1... | collective-permute-start | bytes 491528 | tf_op jit(solution)/shard_map/ppermute | solution.py:23
  8.5 3.1 %collective-permute-start = (bf16[40,2048]{1,0:T(8,128)(2,1)S(1)}, bf16[40,2048]{1,0:T(8,128)(2,1)S(1)}, u32[]{:S(2)}, u32[]{:S(2)}) collective-permute-start(bf16[40,2048]{1,0:T(8,128)(2,1)S(1)} %pad_maximum_fusion.1.refs_0_), channel_id=1, source_target_pairs={{0,112},{16,0},{32,16},{48,32},{64,48},{80,64},{96,80},{112,96},{1... | collective-permute-start | bytes 491528 | tf_op jit(solution)/shard_map/ppermute | solution.py:23
  11.7 2.3 %collective-permute-done.1.refs_2_ = bf16[40,2048]{1,0:T(8,128)(2,1)S(1)} collective-permute-done((bf16[40,2048]{1,0:T(8,128)(2,1)S(1)}, bf16[40,2048]{1,0:T(8,128)(2,1)S(1)}, u32[]{:S(2)}, u32[]{:S(2)}) %collective-permute-start.1) | collective-permute-done | bytes 163872 | tf_op jit(solution)/shard_map/ppermute | solution.py:23
  13.9 4.1 %collective-permute-start.2 = (bf16[40,2048]{1,0:T(8,128)(2,1)S(1)}, bf16[40,2048]{1,0:T(8,128)(2,1)S(1)}, u32[]{:S(2)}, u32[]{:S(2)}) collective-permute-start(bf16[40,2048]{1,0:T(8,128)(2,1)S(1)} %collective-permute-done.1.refs_2_), channel_id=1, source_target_pairs={{0,112},{16,0},{32,16},{48,32},{64,48},{80,64},{96,80},{112,96},{1... | collective-permute-start | bytes 491528 | tf_op jit(solution)/shard_map/ppermute | solution.py:23
  18.0 1.5 collective-permute-start.6
  19.6 3.6 %collective-permute-start.5 = (bf16[40,1024]{1,0:T(8,128)(2,1)S(1)}, bf16[40,1024]{1,0:T(8,128)(2,1)S(1)}, u32[]{:S(2)}, u32[]{:S(2)}) collective-permute-start(bf16[40,1024]{1,0:T(8,128)(2,1)S(1)} %slice.9), channel_id=1, source_target_pairs={{0,96},{16,112},{32,0},{48,16},{64,32},{80,48},{96,64},{112,80},{1... | collective-permute-start | bytes 245768 | tf_op jit(solution)/shard_map/ppermute | solution.py:23
  23.3 4.2 %collective-permute-done.4.refs_4_ = bf16[40,1024]{1,0:T(8,128)(2,1)S(1)} collective-permute-done((bf16[40,1024]{1,0:T(8,128)(2,1)S(1)}, bf16[40,1024]{1,0:T(8,128)(2,1)S(1)}, u32[]{:S(2)}, u32[]{:S(2)}) %collective-permute-start.4) | collective-permute-done | bytes 81952 | tf_op jit(solution)/shard_map/ppermute | solution.py:23
  27.5 1.9 %shard_map.92 = (bf16[160,2048]{1,0:T(8,128)(2,1)S(1)}, bf16[160,2048]{1,0:T(8,128)(2,1)S(1)}, bf16[4,160,1024]{2,1,0:T(8,128)(2,1)}, bf16[4,160,512]{2,1,0:T(8,128)(2,1)}) custom-call(bf16[40,2048]{1,0:T(8,128)(2,1)S(1)} %pad_maximum_fusion.1.refs_0_, bf16[40,2048]{1,0:T(8,128)(2,1)S(1)} %collective-permute-done.refs_1_, ...), custom_call_target="tpu_custom_call" | custom-call | tf_op jit(solution)/shard_map/pallas_call | solution.py:59
  29.4 6.7 %shard_map.94 = f32[160,2688]{1,0:T(8,128)S(1)} custom-call(s32[1]{0:T(128)} %bitcast.1.which, bf16[160,2048]{1,0:T(8,128)(2,1)S(1)} %get-tuple-element.46.feat, bf16[160,2048]{1,0:T(8,128)(2,1)S(1)} %get-tuple-element.47.upst, bf16[2048,1792]{1,0:T(8,128)(2,1)} %gate.5, bf16[2048,1792]{1,0:T(8,128)(2,1)} %up.5, bf16[1792,2048]{1,0:T(8,128)(2,1)} %down.5), custom_call_target="tpu_custom_call" | custom-call | flops 1761607680 | bytes 11010048 | tf_op jit(solution)/shard_map/pallas_call | solution.py:129
  36.1 3.4 %collective-permute-start.8 = (f32[160,2688]{1,0:T(8,128)S(1)}, f32[160,2688]{1,0:T(8,128)}, u32[]{:S(2)}, u32[]{:S(2)}) collective-permute-start(f32[160,2688]{1,0:T(8,128)S(1)} %shard_map.94), channel_id=1, source_target_pairs={{0,128},{128,0},{1,129},{129,1},{2,130},{130,2},{3,131},{131,3},{4... | collective-permute-start | bytes 5160968 | tf_op jit(solution)/shard_map/ppermute | solution.py:37
  39.4 4.3 %all-to-all-start.1 = ((bf16[4,160,1024]{2,1,0:T(8,128)(2,1)}), bf16[4,160,1024]{2,1,0:T(8,128)(2,1)}, u32[]{:S(2)}, u32[]{:S(2)}) async-start(bf16[4,160,1024]{2,1,0:T(8,128)(2,1)} %get-tuple-element.62), calls=%async_computation.1 | async-start | bytes 2621440 | tf_op jit(solution)/shard_map/all_to_all | solution.py:41
  43.7 6.8 %shard_map.93.own = f32[160,2688]{1,0:T(8,128)S(1)} custom-call(s32[1]{0:T(128)} %bitcast.which, bf16[160,2048]{1,0:T(8,128)(2,1)S(1)} %get-tuple-element.46.feat, bf16[160,2048]{1,0:T(8,128)(2,1)S(1)} %get-tuple-element.47.upst, bf16[2048,1792]{1,0:T(8,128)(2,1)} %gate.5, bf16[2048,1792]{1,0:T(8,128)(2,1)} %up.5, bf16[1792,2048]{1,0:T(8,128)(2,1)} %down.5), custom_call_target="tpu_custom_call" | custom-call | flops 1761607680 | bytes 11010048 | tf_op jit(solution)/shard_map/pallas_call | solution.py:129
  50.5 2.7 %shard_map.95 = (bf16[160,1408]{1,0:T(8,128)(2,1)}, bf16[160,1280]{1,0:T(8,128)(2,1)}) custom-call(f32[160,2688]{1,0:T(8,128)S(1)} %shard_map.93.own, f32[160,2688]{1,0:T(8,128)} %collective-permute-done.8.theirs), custom_call_target="tpu_custom_call" | custom-call | tf_op jit(solution)/shard_map/pallas_call | solution.py:59
  53.2 1.3 collective-permute-start.10
  54.5 1.4 collective-permute-start.9
  55.9 0.9 collective-permute-start.11
  56.8 1.0 collective-permute-start.13
  58.0 7.9 %collective-permute-done.10.refs_1_ = bf16[160,1280]{1,0:T(8,128)(2,1)} collective-permute-done((bf16[160,1280]{1,0:T(8,128)(2,1)}, bf16[160,1280]{1,0:T(8,128)(2,1)}, u32[]{:S(2)}, u32[]{:S(2)}) %collective-permute-start.10) | collective-permute-done | bytes 409632 | tf_op jit(solution)/shard_map/ppermute | solution.py:33
  65.9 1.4 collective-permute-start.14
  67.4 1.1 collective-permute-start.16
  68.5 7.9 %collective-permute-done.14.refs_2_ = bf16[160,1280]{1,0:T(8,128)(2,1)S(1)} collective-permute-done((bf16[160,1280]{1,0:T(8,128)(2,1)}, bf16[160,1280]{1,0:T(8,128)(2,1)S(1)}, u32[]{:S(2)}, u32[]{:S(2)}) %collective-permute-start.14) | collective-permute-done | bytes 409632 | tf_op jit(solution)/shard_map/ppermute | solution.py:33
  76.4 0.9 copy-done.5
  77.4 3.8 %all-to-all-start.2 = ((bf16[4,160,512]{2,1,0:T(8,128)(2,1)}), bf16[4,160,512]{2,1,0:T(8,128)(2,1)S(1)}, u32[]{:S(2)}, u32[]{:S(2)}) async-start(bf16[4,160,512]{2,1,0:T(8,128)(2,1)} %get-tuple-element.74), calls=%async_computation.2 | async-start | bytes 1310720 | tf_op jit(solution)/shard_map/all_to_all | solution.py:41
  81.2 13.7 %shard_map.96 = (bf16[8,20,2048]{2,1,0:T(8,128)(2,1)S(1)}, bf16[8,20,2048]{2,1,0:T(8,128)(2,1)S(1)}) custom-call(s32[2]{0:T(128)S(1)} %pad_add_fusion.place, bf16[160,1408]{1,0:T(8,128)(2,1)} %get-tuple-element.50.a_own.refs_0_, bf16[160,1280]{1,0:T(8,128)(2,1)} %get-tuple-element.51.b_own.refs_0_, bf16[160,1408]{1,0:T(8,128)(2,1)} %copy-done.4, ...), custom_call_target="tpu_custom_call" | custom-call | flops 3523215360 | bytes 22020096 | tf_op jit(solution)/shard_map/pallas_call | solution.py:206
  94.9 1.3 pad_maximum_fusion
  96.2 3.7 %all-to-all-start = ((bf16[8,20,4096]{2,1,0:T(8,128)(2,1)}), bf16[8,20,4096]{2,1,0:T(8,128)(2,1)S(1)}, u32[]{:S(2)}, u32[]{:S(2)}) async-start(bf16[8,20,4096]{2,1,0:T(8,128)(2,1)} %pad_maximum_fusion), calls=%async_computation | async-start | bytes 3145728 | tf_op jit(solution)/shard_map/all_to_all | solution.py:410
  99.9 2.3 %collective-permute-start.23 = (bf16[4,160,512]{2,1,0:T(8,128)(2,1)S(1)}, bf16[4,160,512]{2,1,0:T(8,128)(2,1)}, u32[]{:S(2)}, u32[]{:S(2)}) collective-permute-start(bf16[4,160,512]{2,1,0:T(8,128)(2,1)S(1)} %all-to-all-done.2.refs_4_), channel_id=1, source_target_pairs={{0,128},{128,0},{1,129},{129,1},{2,130},{130,2},{3,131},{131,3},{4... | collective-permute-start | bytes 1966088 | tf_op jit(solution)/shard_map/ppermute | solution.py:37
  102.3 1.0 collective-permute-start.15
  103.3 1.7 %collective-permute-start.22 = (bf16[160,1280]{1,0:T(8,128)(2,1)}, bf16[160,1280]{1,0:T(8,128)(2,1)}, u32[]{:S(2)}, u32[]{:S(2)}) collective-permute-start(bf16[160,1280]{1,0:T(8,128)(2,1)} %collective-permute-done.10.refs_1_), channel_id=1, source_target_pairs={{0,4},{1,5},{2,6},{3,7},{4,8},{5,9},{6,10},{7,11},{8,12},{9,13},{1... | collective-permute-start | bytes 1228808 | tf_op jit(solution)/shard_map/ppermute | solution.py:33
  105.1 10.6 %collective-permute-done.15.refs_3_ = bf16[160,1408]{1,0:T(8,128)(2,1)} collective-permute-done((bf16[160,1408]{1,0:T(8,128)(2,1)}, bf16[160,1408]{1,0:T(8,128)(2,1)}, u32[]{:S(2)}, u32[]{:S(2)}) %collective-permute-start.15) | collective-permute-done | bytes 450592 | tf_op jit(solution)/shard_map/ppermute | solution.py:28
  115.7 3.1 %shard_map.99 = (bf16[128,1408]{1,0:T(8,128)(2,1)S(1)}, bf16[128,1408]{1,0:T(8,128)(2,1)S(1)}) custom-call(s32[2]{0:T(128)S(1)} %pad_add_fusion.1.place, bf16[160,1408]{1,0:T(8,128)(2,1)} %get-tuple-element.50.a_own.refs_0_, bf16[160,1408]{1,0:T(8,128)(2,1)} %copy-done.2, bf16[160,1408]{1,0:T(8,128)(2,1)} %copy-done.3, ...), custom_call_target="tpu_custom_call" | custom-call | flops 922746880 | bytes 2457600 | tf_op jit(solution)/shard_map/pallas_call | solution.py:267
  118.9 1.8 %collective-permute-start.17 = (bf16[128,1408]{1,0:T(8,128)(2,1)S(1)}, bf16[128,1408]{1,0:T(8,128)(2,1)S(1)}, u32[]{:S(2)}, u32[]{:S(2)}) collective-permute-start(bf16[128,1408]{1,0:T(8,128)(2,1)S(1)} %get-tuple-element.66), channel_id=1, source_target_pairs={{0,4},{1,5},{2,6},{3,7},{4,8},{5,9},{6,10},{7,11},{8,12},{9,13},{1... | collective-permute-start | bytes 1081352 | tf_op jit(solution)/shard_map/ppermute | solution.py:33
  120.7 1.3 collective-permute-start.18
  122.1 2.9 %shard_map.103 = (bf16[128,1280]{1,0:T(8,128)(2,1)S(1)}, bf16[128,1280]{1,0:T(8,128)(2,1)S(1)}) custom-call(s32[2]{0:T(128)S(1)} %pad_add_fusion.2.place, bf16[160,1280]{1,0:T(8,128)(2,1)} %get-tuple-element.51.b_own.refs_0_, bf16[160,1280]{1,0:T(8,128)(2,1)} %collective-permute-done.10.refs_1_, bf16[160,1280]{1,0:T(8,128)(2,1)} %copy-done.5, ...), custom_call_target="tpu_custom_call" | custom-call | flops 838860800 | bytes 1966080 | tf_op jit(solution)/shard_map/pallas_call | solution.py:267
  125.0 2.7 %collective-permute-start.25 = (bf16[128,1280]{1,0:T(8,128)(2,1)S(1)}, bf16[128,1280]{1,0:T(8,128)(2,1)S(1)}, u32[]{:S(2)}, u32[]{:S(2)}) collective-permute-start(bf16[128,1280]{1,0:T(8,128)(2,1)S(1)} %get-tuple-element.79), channel_id=1, source_target_pairs={{0,3},{1,0},{2,1},{3,2},{4,7},{5,4},{6,5},{7,6},{8,11},{9,8},{10,9... | collective-permute-start | bytes 983048 | tf_op jit(solution)/shard_map/ppermute | solution.py:28
  127.7 5.0 %shard_map.98 = (f32[256,1408]{1,0:T(8,128)S(1)}, f32[256,1408]{1,0:T(8,128)S(1)}, f32[256,1408]{1,0:T(8,128)S(1)}) custom-call(s32[2]{0:T(128)S(1)} %pad_add_fusion.1.place, bf16[160,1408]{1,0:T(8,128)(2,1)} %get-tuple-element.50.a_own.refs_0_, bf16[160,1408]{1,0:T(8,128)(2,1)} %copy-done.2, bf16[160,1408]{1,0:T(8,128)(2,1)} %copy-done.3, ...), custom_call_target="tpu_custom_call" | custom-call | flops 1384120320 | bytes 3768320 | tf_op jit(solution)/shard_map/pallas_call | solution.py:267
  133.2 2.5 %collective-permute-start.20 = (bf16[256,1408]{1,0:T(8,128)(2,1)S(1)}, bf16[256,1408]{1,0:T(8,128)(2,1)S(1)}, u32[]{:S(2)}, u32[]{:S(2)}) collective-permute-start(bf16[256,1408]{1,0:T(8,128)(2,1)S(1)} %get-tuple-element.69), channel_id=1, source_target_pairs={{0,12},{1,13},{2,14},{3,15},{4,0},{5,1},{6,2},{7,3},{8,4},{9,5},{1... | collective-permute-start | bytes 2162696 | tf_op jit(solution)/shard_map/ppermute | solution.py:33
  135.7 4.2 %shard_map.102 = (f32[256,1280]{1,0:T(8,128)S(1)}, f32[256,1280]{1,0:T(8,128)S(1)}, f32[256,1280]{1,0:T(8,128)S(1)}) custom-call(s32[2]{0:T(128)S(1)} %pad_add_fusion.2.place, bf16[160,1280]{1,0:T(8,128)(2,1)} %get-tuple-element.51.b_own.refs_0_, bf16[160,1280]{1,0:T(8,128)(2,1)} %collective-permute-done.10.refs_1_, bf16[160,1280]{1,0:T(8,128)(2,1)} %copy-done.5, ...), custom_call_target="tpu_custom_call" | custom-call | flops 1258291200 | bytes 2621440 | tf_op jit(solution)/shard_map/pallas_call | solution.py:267
  140.2 2.7 %collective-permute-start.27 = (bf16[256,1280]{1,0:T(8,128)(2,1)S(1)}, bf16[256,1280]{1,0:T(8,128)(2,1)S(1)}, u32[]{:S(2)}, u32[]{:S(2)}) collective-permute-start(bf16[256,1280]{1,0:T(8,128)(2,1)S(1)} %get-tuple-element.81), channel_id=1, source_target_pairs={{0,3},{1,0},{2,1},{3,2},{4,7},{5,4},{6,5},{7,6},{8,11},{9,8},{10,9... | collective-permute-start | bytes 1966088 | tf_op jit(solution)/shard_map/ppermute | solution.py:28
  142.9 7.3 %collective-permute-done.19.from_before = bf16[256,1408]{1,0:T(8,128)(2,1)S(1)} collective-permute-done((bf16[256,1408]{1,0:T(8,128)(2,1)S(1)}, bf16[256,1408]{1,0:T(8,128)(2,1)S(1)}, u32[]{:S(2)}, u32[]{:S(2)}) %collective-permute-start.19) | collective-permute-done | bytes 720928 | tf_op jit(solution)/shard_map/ppermute | solution.py:33
  150.4 2.7 %collective-permute-start.21 = (bf16[128,1408]{1,0:T(8,128)(2,1)S(1)}, bf16[128,1408]{1,0:T(8,128)(2,1)S(1)}, u32[]{:S(2)}, u32[]{:S(2)}) collective-permute-start(bf16[128,1408]{1,0:T(8,128)(2,1)S(1)} %get-tuple-element.71), channel_id=1, source_target_pairs={{0,128},{128,0},{1,129},{129,1},{2,130},{130,2},{3,131},{131,3},{4... | collective-permute-start | bytes 1081352 | tf_op jit(solution)/shard_map/ppermute | solution.py:37
  153.1 2.2 %collective-permute-done.26.from_before = bf16[256,1280]{1,0:T(8,128)(2,1)S(1)} collective-permute-done((bf16[256,1280]{1,0:T(8,128)(2,1)S(1)}, bf16[256,1280]{1,0:T(8,128)(2,1)S(1)}, u32[]{:S(2)}, u32[]{:S(2)}) %collective-permute-start.26) | collective-permute-done | bytes 655392 | tf_op jit(solution)/shard_map/ppermute | solution.py:28
  155.4 0.8 shard_map.105
  156.2 3.2 %collective-permute-start.28 = (bf16[128,1280]{1,0:T(8,128)(2,1)}, bf16[128,1280]{1,0:T(8,128)(2,1)S(1)}, u32[]{:S(2)}, u32[]{:S(2)}) collective-permute-start(bf16[128,1280]{1,0:T(8,128)(2,1)} %get-tuple-element.83), channel_id=1, source_target_pairs={{0,128},{128,0},{1,129},{129,1},{2,130},{130,2},{3,131},{131,3},{4... | collective-permute-start | bytes 983048 | tf_op jit(solution)/shard_map/ppermute | solution.py:37
  159.4 0.8 shard_map.97
  160.2 0.6 collective-permute-done.28.other_b
  160.9 1.3 shard_map.106
  (50 shorter events, 1.7 us)
Async XLA Ops:
  1.6 12.3 %collective-permute-start.1 = (bf16[40,2048]{1,0:T(8,128)(2,1)S(1)}, bf16[40,2048]{1,0:T(8,128)(2,1)S(1)}, u32[]{:S(2)}, u32[]{:S(2)}) collective-permute-start(bf16[40,2048]{1,0:T(8,128)(2,1)S(1)} %pad_maximum_fusion.1.refs_0_), channel_id=1, source_target_pairs={{0,96},{16,112},{32,0},{48,16},{64,32},{80,48},{96,64},{112,80},{1... | collective-permute-start | bytes 491528 | tf_op jit(solution)/shard_map/ppermute | solution.py:23
  8.5 9.5 %collective-permute-start.3 = (bf16[40,2048]{1,0:T(8,128)(2,1)S(1)}, bf16[40,2048]{1,0:T(8,128)(2,1)S(1)}, u32[]{:S(2)}, u32[]{:S(2)}) collective-permute-start(bf16[40,2048]{1,0:T(8,128)(2,1)S(1)} %pad_maximum_fusion.1.refs_0_), channel_id=1, source_target_pairs={{0,32},{16,48},{32,64},{48,80},{64,96},{80,112},{96,0},{112,16},{1... | collective-permute-start | bytes 491528 | tf_op jit(solution)/shard_map/ppermute | solution.py:23
  8.5 11.1 %collective-permute-start = (bf16[40,2048]{1,0:T(8,128)(2,1)S(1)}, bf16[40,2048]{1,0:T(8,128)(2,1)S(1)}, u32[]{:S(2)}, u32[]{:S(2)}) collective-permute-start(bf16[40,2048]{1,0:T(8,128)(2,1)S(1)} %pad_maximum_fusion.1.refs_0_), channel_id=1, source_target_pairs={{0,112},{16,0},{32,16},{48,32},{64,48},{80,64},{96,80},{112,96},{1... | collective-permute-start | bytes 491528 | tf_op jit(solution)/shard_map/ppermute | solution.py:23
  11.7 11.6 %collective-permute-start.7 = (bf16[40,2048]{1,0:T(8,128)(2,1)S(1)}, bf16[40,2048]{1,0:T(8,128)(2,1)S(1)}, u32[]{:S(2)}, u32[]{:S(2)}) collective-permute-start(bf16[40,2048]{1,0:T(8,128)(2,1)S(1)} %pad_maximum_fusion.1.refs_0_), channel_id=1, source_target_pairs={{0,16},{16,32},{32,48},{48,64},{64,80},{80,96},{96,112},{112,0},{1... | collective-permute-start | bytes 491528 | tf_op jit(solution)/shard_map/ppermute | solution.py:23
  13.9 13.6 %collective-permute-start.2 = (bf16[40,2048]{1,0:T(8,128)(2,1)S(1)}, bf16[40,2048]{1,0:T(8,128)(2,1)S(1)}, u32[]{:S(2)}, u32[]{:S(2)}) collective-permute-start(bf16[40,2048]{1,0:T(8,128)(2,1)S(1)} %collective-permute-done.1.refs_2_), channel_id=1, source_target_pairs={{0,112},{16,0},{32,16},{48,32},{64,48},{80,64},{96,80},{112,96},{1... | collective-permute-start | bytes 491528 | tf_op jit(solution)/shard_map/ppermute | solution.py:23
  18.0 9.4 %collective-permute-start.6 = (bf16[40,2048]{1,0:T(8,128)(2,1)S(1)}, bf16[40,2048]{1,0:T(8,128)(2,1)S(1)}, u32[]{:S(2)}, u32[]{:S(2)}) collective-permute-start(bf16[40,2048]{1,0:T(8,128)(2,1)S(1)} %collective-permute-done.3.refs_7_), channel_id=1, source_target_pairs={{0,16},{16,32},{32,48},{48,64},{64,80},{80,96},{96,112},{112,0},{1... | collective-permute-start | bytes 491528 | tf_op jit(solution)/shard_map/ppermute | solution.py:23
  19.6 7.9 %collective-permute-start.4 = (bf16[40,1024]{1,0:T(8,128)(2,1)S(1)}, bf16[40,1024]{1,0:T(8,128)(2,1)S(1)}, u32[]{:S(2)}, u32[]{:S(2)}) collective-permute-start(bf16[40,1024]{1,0:T(8,128)(2,1)S(1)} %slice.8), channel_id=1, source_target_pairs={{0,32},{16,48},{32,64},{48,80},{64,96},{80,112},{96,0},{112,16},{1... | collective-permute-start | bytes 245768 | tf_op jit(solution)/shard_map/ppermute | solution.py:23
  19.6 7.9 %collective-permute-start.5 = (bf16[40,1024]{1,0:T(8,128)(2,1)S(1)}, bf16[40,1024]{1,0:T(8,128)(2,1)S(1)}, u32[]{:S(2)}, u32[]{:S(2)}) collective-permute-start(bf16[40,1024]{1,0:T(8,128)(2,1)S(1)} %slice.9), channel_id=1, source_target_pairs={{0,96},{16,112},{32,0},{48,16},{64,32},{80,48},{96,64},{112,80},{1... | collective-permute-start | bytes 245768 | tf_op jit(solution)/shard_map/ppermute | solution.py:23
  36.1 14.4 %collective-permute-start.8 = (f32[160,2688]{1,0:T(8,128)S(1)}, f32[160,2688]{1,0:T(8,128)}, u32[]{:S(2)}, u32[]{:S(2)}) collective-permute-start(f32[160,2688]{1,0:T(8,128)S(1)} %shard_map.94), channel_id=1, source_target_pairs={{0,128},{128,0},{1,129},{129,1},{2,130},{130,2},{3,131},{131,3},{4... | collective-permute-start | bytes 5160968 | tf_op jit(solution)/shard_map/ppermute | solution.py:37
  39.4 28.0 %all-to-all-start.1 = ((bf16[4,160,1024]{2,1,0:T(8,128)(2,1)}), bf16[4,160,1024]{2,1,0:T(8,128)(2,1)}, u32[]{:S(2)}, u32[]{:S(2)}) async-start(bf16[4,160,1024]{2,1,0:T(8,128)(2,1)} %get-tuple-element.62), calls=%async_computation.1 | async-start | bytes 2621440 | tf_op jit(solution)/shard_map/all_to_all | solution.py:41
  53.2 12.7 %collective-permute-start.10 = (bf16[160,1280]{1,0:T(8,128)(2,1)}, bf16[160,1280]{1,0:T(8,128)(2,1)}, u32[]{:S(2)}, u32[]{:S(2)}) collective-permute-start(bf16[160,1280]{1,0:T(8,128)(2,1)} %get-tuple-element.51.b_own.refs_0_), channel_id=1, source_target_pairs={{0,4},{1,5},{2,6},{3,7},{4,8},{5,9},{6,10},{7,11},{8,12},{9,13},{1... | collective-permute-start | bytes 1228808 | tf_op jit(solution)/shard_map/ppermute | solution.py:33
  54.5 21.9 %collective-permute-start.9 = (bf16[160,1408]{1,0:T(8,128)(2,1)}, bf16[160,1408]{1,0:T(8,128)(2,1)S(1)}, u32[]{:S(2)}, u32[]{:S(2)}) collective-permute-start(bf16[160,1408]{1,0:T(8,128)(2,1)} %get-tuple-element.50.a_own.refs_0_), channel_id=1, source_target_pairs={{0,1},{1,2},{2,3},{3,0},{4,5},{5,6},{6,7},{7,4},{8,9},{9,10},{10,1... | collective-permute-start | bytes 1351688 | tf_op jit(solution)/shard_map/ppermute | solution.py:28
  55.9 20.5 %collective-permute-start.11 = (bf16[160,1408]{1,0:T(8,128)(2,1)}, bf16[160,1408]{1,0:T(8,128)(2,1)S(1)}, u32[]{:S(2)}, u32[]{:S(2)}) collective-permute-start(bf16[160,1408]{1,0:T(8,128)(2,1)} %get-tuple-element.50.a_own.refs_0_), channel_id=1, source_target_pairs={{0,128},{128,0},{1,129},{129,1},{2,130},{130,2},{3,131},{131,3},{4... | collective-permute-start | bytes 1351688 | tf_op jit(solution)/shard_map/ppermute | solution.py:37
  56.8 19.6 %collective-permute-start.13 = (bf16[160,1408]{1,0:T(8,128)(2,1)}, bf16[160,1408]{1,0:T(8,128)(2,1)S(1)}, u32[]{:S(2)}, u32[]{:S(2)}) collective-permute-start(bf16[160,1408]{1,0:T(8,128)(2,1)} %get-tuple-element.50.a_own.refs_0_), channel_id=1, source_target_pairs={{0,3},{1,0},{2,1},{3,2},{4,7},{5,4},{6,5},{7,6},{8,11},{9,8},{10,9... | collective-permute-start | bytes 1351688 | tf_op jit(solution)/shard_map/ppermute | solution.py:28
  57.8 9.6 %collective-permute-start.12 = (bf16[160,1280]{1,0:T(8,128)(2,1)}, bf16[160,1280]{1,0:T(8,128)(2,1)}, u32[]{:S(2)}, u32[]{:S(2)}) collective-permute-start(bf16[160,1280]{1,0:T(8,128)(2,1)} %get-tuple-element.51.b_own.refs_0_), channel_id=1, source_target_pairs={{0,128},{128,0},{1,129},{129,1},{2,130},{130,2},{3,131},{131,3},{4... | collective-permute-start | bytes 1228808 | tf_op jit(solution)/shard_map/ppermute | solution.py:37
  65.9 10.5 %collective-permute-start.14 = (bf16[160,1280]{1,0:T(8,128)(2,1)}, bf16[160,1280]{1,0:T(8,128)(2,1)S(1)}, u32[]{:S(2)}, u32[]{:S(2)}) collective-permute-start(bf16[160,1280]{1,0:T(8,128)(2,1)} %get-tuple-element.51.b_own.refs_0_), channel_id=1, source_target_pairs={{0,12},{1,13},{2,14},{3,15},{4,0},{5,1},{6,2},{7,3},{8,4},{9,5},{1... | collective-permute-start | bytes 1228808 | tf_op jit(solution)/shard_map/ppermute | solution.py:33
  67.4 37.7 %collective-permute-start.16 = (bf16[4,160,1024]{2,1,0:T(8,128)(2,1)}, bf16[4,160,1024]{2,1,0:T(8,128)(2,1)S(1)}, u32[]{:S(2)}, u32[]{:S(2)}) collective-permute-start(bf16[4,160,1024]{2,1,0:T(8,128)(2,1)} %all-to-all-done.1.refs_4_), channel_id=1, source_target_pairs={{0,128},{128,0},{1,129},{129,1},{2,130},{130,2},{3,131},{131,3},{4... | collective-permute-start | bytes 3932168 | tf_op jit(solution)/shard_map/ppermute | solution.py:37
  76.4 1.0 copy-start.5
  76.4 18.5 %copy-start.2 = (bf16[160,1408]{1,0:T(8,128)(2,1)}, bf16[160,1408]{1,0:T(8,128)(2,1)S(1)}, u32[]{:S(2)}) copy-start(bf16[160,1408]{1,0:T(8,128)(2,1)S(1)} %collective-permute-done.9.refs_1_) | copy-start | bytes 1351684
  76.4 4.8 %copy-start.4 = (bf16[160,1408]{1,0:T(8,128)(2,1)}, bf16[160,1408]{1,0:T(8,128)(2,1)S(1)}, u32[]{:S(2)}) copy-start(bf16[160,1408]{1,0:T(8,128)(2,1)S(1)} %collective-permute-done.11.a_theirs) | copy-start | bytes 1351684
  76.4 18.5 %copy-start.3 = (bf16[160,1408]{1,0:T(8,128)(2,1)}, bf16[160,1408]{1,0:T(8,128)(2,1)S(1)}, u32[]{:S(2)}) copy-start(bf16[160,1408]{1,0:T(8,128)(2,1)S(1)} %collective-permute-done.13.refs_2_) | copy-start | bytes 1351684
  77.4 18.9 %all-to-all-start.2 = ((bf16[4,160,512]{2,1,0:T(8,128)(2,1)}), bf16[4,160,512]{2,1,0:T(8,128)(2,1)S(1)}, u32[]{:S(2)}, u32[]{:S(2)}) async-start(bf16[4,160,512]{2,1,0:T(8,128)(2,1)} %get-tuple-element.74), calls=%async_computation.2 | async-start | bytes 1310720 | tf_op jit(solution)/shard_map/all_to_all | solution.py:41
  96.2 3.7 %copy-start.1 = (bf16[4,160,512]{2,1,0:T(8,128)(2,1)}, bf16[4,160,512]{2,1,0:T(8,128)(2,1)S(1)}, u32[]{:S(2)}) copy-start(bf16[4,160,512]{2,1,0:T(8,128)(2,1)S(1)} %all-to-all-done.2.refs_4_) | copy-start | bytes 1966084
  96.2 63.2 %all-to-all-start = ((bf16[8,20,4096]{2,1,0:T(8,128)(2,1)}), bf16[8,20,4096]{2,1,0:T(8,128)(2,1)S(1)}, u32[]{:S(2)}, u32[]{:S(2)}) async-start(bf16[8,20,4096]{2,1,0:T(8,128)(2,1)} %pad_maximum_fusion), calls=%async_computation | async-start | bytes 3145728 | tf_op jit(solution)/shard_map/all_to_all | solution.py:410
  99.9 22.1 %collective-permute-start.23 = (bf16[4,160,512]{2,1,0:T(8,128)(2,1)S(1)}, bf16[4,160,512]{2,1,0:T(8,128)(2,1)}, u32[]{:S(2)}, u32[]{:S(2)}) collective-permute-start(bf16[4,160,512]{2,1,0:T(8,128)(2,1)S(1)} %all-to-all-done.2.refs_4_), channel_id=1, source_target_pairs={{0,128},{128,0},{1,129},{129,1},{2,130},{130,2},{3,131},{131,3},{4... | collective-permute-start | bytes 1966088 | tf_op jit(solution)/shard_map/ppermute | solution.py:37
  102.3 13.4 %collective-permute-start.15 = (bf16[160,1408]{1,0:T(8,128)(2,1)}, bf16[160,1408]{1,0:T(8,128)(2,1)}, u32[]{:S(2)}, u32[]{:S(2)}) collective-permute-start(bf16[160,1408]{1,0:T(8,128)(2,1)} %copy-done.2), channel_id=1, source_target_pairs={{0,1},{1,2},{2,3},{3,0},{4,5},{5,6},{6,7},{7,4},{8,9},{9,10},{10,1... | collective-permute-start | bytes 1351688 | tf_op jit(solution)/shard_map/ppermute | solution.py:28
  103.3 18.8 %collective-permute-start.22 = (bf16[160,1280]{1,0:T(8,128)(2,1)}, bf16[160,1280]{1,0:T(8,128)(2,1)}, u32[]{:S(2)}, u32[]{:S(2)}) collective-permute-start(bf16[160,1280]{1,0:T(8,128)(2,1)} %collective-permute-done.10.refs_1_), channel_id=1, source_target_pairs={{0,4},{1,5},{2,6},{3,7},{4,8},{5,9},{6,10},{7,11},{8,12},{9,13},{1... | collective-permute-start | bytes 1228808 | tf_op jit(solution)/shard_map/ppermute | solution.py:33
  105.1 10.6 %copy-start = (bf16[4,160,1024]{2,1,0:T(8,128)(2,1)}, bf16[4,160,1024]{2,1,0:T(8,128)(2,1)S(1)}, u32[]{:S(2)}) copy-start(bf16[4,160,1024]{2,1,0:T(8,128)(2,1)S(1)} %collective-permute-done.16.refs_5_) | copy-start | bytes 3932164
  118.9 13.8 %collective-permute-start.17 = (bf16[128,1408]{1,0:T(8,128)(2,1)S(1)}, bf16[128,1408]{1,0:T(8,128)(2,1)S(1)}, u32[]{:S(2)}, u32[]{:S(2)}) collective-permute-start(bf16[128,1408]{1,0:T(8,128)(2,1)S(1)} %get-tuple-element.66), channel_id=1, source_target_pairs={{0,4},{1,5},{2,6},{3,7},{4,8},{5,9},{6,10},{7,11},{8,12},{9,13},{1... | collective-permute-start | bytes 1081352 | tf_op jit(solution)/shard_map/ppermute | solution.py:33
  120.7 12.0 %collective-permute-start.18 = (bf16[128,1408]{1,0:T(8,128)(2,1)S(1)}, bf16[128,1408]{1,0:T(8,128)(2,1)S(1)}, u32[]{:S(2)}, u32[]{:S(2)}) collective-permute-start(bf16[128,1408]{1,0:T(8,128)(2,1)S(1)} %get-tuple-element.67), channel_id=1, source_target_pairs={{0,12},{1,13},{2,14},{3,15},{4,0},{5,1},{6,2},{7,3},{8,4},{9,5},{1... | collective-permute-start | bytes 1081352 | tf_op jit(solution)/shard_map/ppermute | solution.py:33
  124.9 15.0 %collective-permute-start.24 = (bf16[128,1280]{1,0:T(8,128)(2,1)S(1)}, bf16[128,1280]{1,0:T(8,128)(2,1)S(1)}, u32[]{:S(2)}, u32[]{:S(2)}) collective-permute-start(bf16[128,1280]{1,0:T(8,128)(2,1)S(1)} %get-tuple-element.78), channel_id=1, source_target_pairs={{0,1},{1,2},{2,3},{3,0},{4,5},{5,6},{6,7},{7,4},{8,9},{9,10},{10,1... | collective-permute-start | bytes 983048 | tf_op jit(solution)/shard_map/ppermute | solution.py:28
  125.0 14.9 %collective-permute-start.25 = (bf16[128,1280]{1,0:T(8,128)(2,1)S(1)}, bf16[128,1280]{1,0:T(8,128)(2,1)S(1)}, u32[]{:S(2)}, u32[]{:S(2)}) collective-permute-start(bf16[128,1280]{1,0:T(8,128)(2,1)S(1)} %get-tuple-element.79), channel_id=1, source_target_pairs={{0,3},{1,0},{2,1},{3,2},{4,7},{5,4},{6,5},{7,6},{8,11},{9,8},{10,9... | collective-permute-start | bytes 983048 | tf_op jit(solution)/shard_map/ppermute | solution.py:28
  132.9 17.2 %collective-permute-start.19 = (bf16[256,1408]{1,0:T(8,128)(2,1)S(1)}, bf16[256,1408]{1,0:T(8,128)(2,1)S(1)}, u32[]{:S(2)}, u32[]{:S(2)}) collective-permute-start(bf16[256,1408]{1,0:T(8,128)(2,1)S(1)} %get-tuple-element.68), channel_id=1, source_target_pairs={{0,4},{1,5},{2,6},{3,7},{4,8},{5,9},{6,10},{7,11},{8,12},{9,13},{1... | collective-permute-start | bytes 2162696 | tf_op jit(solution)/shard_map/ppermute | solution.py:33
  133.2 17.0 %collective-permute-start.20 = (bf16[256,1408]{1,0:T(8,128)(2,1)S(1)}, bf16[256,1408]{1,0:T(8,128)(2,1)S(1)}, u32[]{:S(2)}, u32[]{:S(2)}) collective-permute-start(bf16[256,1408]{1,0:T(8,128)(2,1)S(1)} %get-tuple-element.69), channel_id=1, source_target_pairs={{0,12},{1,13},{2,14},{3,15},{4,0},{5,1},{6,2},{7,3},{8,4},{9,5},{1... | collective-permute-start | bytes 2162696 | tf_op jit(solution)/shard_map/ppermute | solution.py:33
  140.1 15.2 %collective-permute-start.26 = (bf16[256,1280]{1,0:T(8,128)(2,1)S(1)}, bf16[256,1280]{1,0:T(8,128)(2,1)S(1)}, u32[]{:S(2)}, u32[]{:S(2)}) collective-permute-start(bf16[256,1280]{1,0:T(8,128)(2,1)S(1)} %get-tuple-element.80), channel_id=1, source_target_pairs={{0,1},{1,2},{2,3},{3,0},{4,5},{5,6},{6,7},{7,4},{8,9},{9,10},{10,1... | collective-permute-start | bytes 1966088 | tf_op jit(solution)/shard_map/ppermute | solution.py:28
  140.2 15.2 %collective-permute-start.27 = (bf16[256,1280]{1,0:T(8,128)(2,1)S(1)}, bf16[256,1280]{1,0:T(8,128)(2,1)S(1)}, u32[]{:S(2)}, u32[]{:S(2)}) collective-permute-start(bf16[256,1280]{1,0:T(8,128)(2,1)S(1)} %get-tuple-element.81), channel_id=1, source_target_pairs={{0,3},{1,0},{2,1},{3,2},{4,7},{5,4},{6,5},{7,6},{8,11},{9,8},{10,9... | collective-permute-start | bytes 1966088 | tf_op jit(solution)/shard_map/ppermute | solution.py:28
  150.4 9.9 %collective-permute-start.21 = (bf16[128,1408]{1,0:T(8,128)(2,1)S(1)}, bf16[128,1408]{1,0:T(8,128)(2,1)S(1)}, u32[]{:S(2)}, u32[]{:S(2)}) collective-permute-start(bf16[128,1408]{1,0:T(8,128)(2,1)S(1)} %get-tuple-element.71), channel_id=1, source_target_pairs={{0,128},{128,0},{1,129},{129,1},{2,130},{130,2},{3,131},{131,3},{4... | collective-permute-start | bytes 1081352 | tf_op jit(solution)/shard_map/ppermute | solution.py:37
  156.2 4.7 %collective-permute-start.28 = (bf16[128,1280]{1,0:T(8,128)(2,1)}, bf16[128,1280]{1,0:T(8,128)(2,1)S(1)}, u32[]{:S(2)}, u32[]{:S(2)}) collective-permute-start(bf16[128,1280]{1,0:T(8,128)(2,1)} %get-tuple-element.83), channel_id=1, source_target_pairs={{0,128},{128,0},{1,129},{129,1},{2,130},{130,2},{3,131},{131,3},{4... | collective-permute-start | bytes 983048 | tf_op jit(solution)/shard_map/ppermute | solution.py:37

commit v2 on v1

--- a/solution.py
+++ b/solution.py
@@ -13,6 +13,7 @@
 ALONG_X = [[SIDE * y + x for x in range(SIDE)] for y in range(SIDE)]
 ALONG_Y = [[SIDE * y + x for y in range(SIDE)] for x in range(SIDE)]
 MIB = 1 << 20
+PROJECT_STEPS, BACK_STEPS = 8, 4
 
 
 def dot(left, right, dims):
@@ -125,7 +126,7 @@
 def project(which, features, upstream, weights):
     group, model = features.shape
     half = weights[0].shape[1] // 2
-    step = model // 4
+    step = model // PROJECT_STEPS
     return pl.pallas_call(
         project_kernel,
         grid_spec=pltpu.PrefetchScalarGridSpec(
@@ -146,7 +147,7 @@
     )(which, features, upstream, *hbm(*weights))
 
 
-def swiglu_kernel(own, theirs, route_a, route_b):
+def swiglu_kernel(own, theirs, route_a, route_b, grads):
     half = own.shape[1] // 3
     cut = route_a.shape[1] - half
     parts = [slice(half * k, half * (k + 1)) for k in range(3)]
@@ -154,47 +155,47 @@
     up_pre = own[:, parts[1]] + theirs[:, parts[1]]
     hidden_grad = own[:, parts[2]] + theirs[:, parts[2]]
     logistic = jax.nn.sigmoid(gate_pre)
-    route_a[:, :half] = (gate_pre * logistic * up_pre).astype(BF)
+    hidden = (gate_pre * logistic * up_pre).astype(BF)
     gate_grad = hidden_grad * up_pre * logistic * (1.0 + gate_pre * (1.0 - logistic))
     gate_grad = gate_grad.astype(BF)
+    up_grad = (hidden_grad * gate_pre * logistic).astype(BF)
+    route_a[:, :half] = hidden
     route_a[:, half:] = gate_grad[:, :cut]
     route_b[:, : half - cut] = gate_grad[:, cut:]
-    route_b[:, half - cut :] = (hidden_grad * gate_pre * logistic).astype(BF)
-
-
-def back_kernel(place, a_own, b_own, a_theirs, b_theirs, gate, up, down, out, inp, total):
+    route_b[:, half - cut :] = up_grad
+    for part, value in zip(parts, (gate_grad, up_grad, hidden)):
+        grads[:, part] = value
+
+
+def back_kernel(place, own, theirs, gate, up, down, out, total):
     half = down.shape[0]
-    cut = a_own.shape[1] - half
-    rest = half - cut
-    rows = out.shape[1]
+    rows, step = out.shape[1], gate.shape[0]
     inner = pl.program_id(1)
 
-    def add(a, b):
-        first = dot(a[:, :half], down[...], ((1,), (0,)))
-        grads = jnp.concatenate([a[:, half:], b[:, :rest]], axis=1)
-        second = dot(grads, gate[...], ((1,), (1,))) + dot(b[:, rest:], up[...], ((1,), (1,)))
+    def add(grads):
+        first = dot(grads[:, 2 * half :], down[...], ((1,), (0,)))
+        second = dot(grads[:, :half], gate[...], ((1,), (1,)))
+        second = second + dot(grads[:, half : 2 * half], up[...], ((1,), (1,)))
         return first, second
 
     @pl.when(inner == 0)
     def _():
-        total[0], total[1] = add(a_own, b_own)
+        total[:, :step], total[:, step:] = add(own)
 
     @pl.when(inner == 1)
     def _():
-        first, second = add(a_theirs, b_theirs)
-        first = total[0] + first
-        second = total[1] + second
+        first, second = add(theirs)
+        total[:, :step] = total[:, :step] + first
+        total[:, step:] = total[:, step:] + second
         for k in range(COLS):
             at = lax.rem(place[1] + k, COLS)
-            block = slice(rows * k, rows * (k + 1))
-            out[at] = first[block].astype(BF)
-            inp[at] = second[block].astype(BF)
-
-
-def back(place, routes, weights, rows):
+            out[at] = total[pl.ds(rows * k, rows), :].astype(BF)
+
+
+def back(place, grads, weights, rows):
     model, units = weights[0].shape
     half = units // 2
-    step = model // 4
+    step = model // BACK_STEPS
 
     def whole(value):
         return pl.BlockSpec(value.shape, lambda n, j, p: (0, 0))
@@ -202,25 +203,24 @@
     def pick(j, p):
         return lax.rem(p[0] + j, 2)
 
-    block = pl.BlockSpec((COLS, rows, step), lambda n, j, p: (0, 0, n))
     return pl.pallas_call(
         back_kernel,
         grid_spec=pltpu.PrefetchScalarGridSpec(
             num_scalar_prefetch=1,
-            grid=(model // step, 2),
-            in_specs=[whole(r) for r in routes]
+            grid=(BACK_STEPS, 2),
+            in_specs=[whole(g) for g in grads]
             + [
                 pl.BlockSpec((step, half), lambda n, j, p: (n, pick(j, p))),
                 pl.BlockSpec((step, half), lambda n, j, p: (n, pick(j, p))),
                 pl.BlockSpec((half, step), lambda n, j, p: (pick(j, p), n)),
             ],
-            out_specs=[block, block],
-            scratch_shapes=[pltpu.VMEM((2, COLS * rows, step), F32)],
+            out_specs=pl.BlockSpec((COLS, rows, 2 * step), lambda n, j, p: (0, 0, n)),
+            scratch_shapes=[pltpu.VMEM((COLS * rows, 2 * step), F32)],
         ),
-        out_shape=[shape(COLS, rows, model)] * 2,
+        out_shape=shape(COLS, rows, 2 * model),
         cost_estimate=cost(6 * COLS * rows * model * units, 6 * model * units),
         compiler_params=pltpu.CompilerParams(vmem_limit_bytes=20 * MIB),
-    )(place, *hbm(*routes, *weights))
+    )(place, *hbm(*grads, *weights))
 
 
 def weight_kernel(cut, far, place, *refs):
@@ -331,12 +331,14 @@
 
 
 def total_kernel(moved, out, grad):
-    model = out.shape[1]
+    step = out.shape[1] // BACK_STEPS
     total = moved[0].astype(F32)
     for k in range(1, COLS):
         total = total + moved[k].astype(F32)
-    out[...] = total[:, :model].astype(BF)
-    grad[...] = total[:, model:].astype(BF)
+    total = total.astype(BF)
+    for n in range(BACK_STEPS):
+        out[:, step * n : step * (n + 1)] = total[:, 2 * step * n : step * (2 * n + 1)]
+        grad[:, step * n : step * (n + 1)] = total[:, step * (2 * n + 1) : 2 * step * (n + 1)]
 
 
 def gather(value, send):
@@ -385,11 +387,11 @@
     kept = project(jnp.reshape(row, (1,)), features, upstream, weights)
     routes = call(
         swiglu_kernel,
-        [pltpu.HBM((group, half + cut), BF), pltpu.HBM((group, 2 * half - cut), BF)],
+        [pltpu.HBM((group, n), BF) for n in (half + cut, 2 * half - cut, 3 * half)],
         kept,
         *hbm(to_core(sent)),
     )
-    route_a, route_b = routes
+    route_a, route_b, grads = routes
     wide_a = gather(route_a, to_x)
     wide_b = gather(route_b, to_y)
 
@@ -400,13 +402,12 @@
     columns_a = (columns_a, to_core(columns_a))
     columns_b = (columns_b, to_core(columns_b))
 
-    theirs = (to_core(route_a), to_core(route_b))
-    routes, _ = lax.optimization_barrier(
-        ((route_a, route_b, *theirs), (*wide_a[1:3], *wide_b[1:3]))
-    )
-    part = back(jnp.stack([row, col]), routes, weights, rows)
+    grads, _ = lax.optimization_barrier(
+        ((grads, to_core(grads)), (*wide_a[1:3], *wide_b[1:3]))
+    )
+    part = back(jnp.stack([row, col]), grads, weights, rows)
     wide_a[1], wide_b[1], part = lax.optimization_barrier((wide_a[1], wide_b[1], part))
-    part = jnp.concatenate(part, axis=2)
+    part, _ = lax.optimization_barrier((part, (wide_a[3], wide_b[3])))
     moved = lax.all_to_all(part, "col", split_axis=0, concat_axis=0, tiled=True)
     layer_out, input_grad = call(total_kernel, [shape(rows, model)] * 2, moved)
 

time: 163 us -> 152 us (0.933)
  waiting for transfers between devices: 43 us -> 30.3 us
  Pallas kernels: 50.6 us -> 56.1 us
  starting transfers between devices: 64.2 us -> 60.1 us
  local copies, waits for them, and re-layouts: 0.95 us -> 2.77 us
    ppermute x7, waiting for transfers between devices: 23 us -> 9.68 us  [to_y(): lax.ppermute(value, 'depth', [(k, (k + SIDE * step) % side) for k in rang...]
    pallas_call x2, Pallas kernels: 13.4 us -> 18.2 us  [project(): pl.pallas_call(project_kernel, grid_spec=pltpu.PrefetchScalarGridSpec(num...]
    ppermute x7 -> x6, starting transfers between devices: 13.9 us -> 10.2 us  [to_core(): return lax.ppermute(value, 'row', [(0, 1), (1, 0)])]
    unnamed x12 -> x10, local copies, waits for them, and re-layouts: 0.94 us -> 2.76 us
  transfers between devices with their start and end apart: 32 -> 31, of which waited for: 8 -> 8; matrix products, arithmetic and copies ran while one was open for 1% -> 0% of each run, Pallas kernels for 25% -> 29%
where the time goes in v2:
time: 152 us; the launch traced here: 151 us
  starting transfers between devices  60.1 us (40%)
  Pallas kernels  56.1 us (37%)
  waiting for transfers between devices  30.3 us (20%)
  local copies, waits for them, and re-layouts  2.77 us (2%)
    ppermute x8, starting transfers between devices, to_z(): lax.ppermute(value, 'col', [(k, (k + step) % COLS) for k in range(COLS)])  19.3 us
    pallas_call x2, Pallas kernels, project(): pl.pallas_call(project_kernel, grid_spec=pltpu.PrefetchScalarGridSpec(num...  18.2 us
    pallas_call x4, Pallas kernels, weight_partials(): pl.pallas_call(functools.partial(weight_kernel, cut, far), in_specs=[pl.B...  15.2 us
    pallas_call x1, Pallas kernels, back(): pl.pallas_call(back_kernel, grid_spec=pltpu.PrefetchScalarGridSpec(num_sc...  14.8 us
    ppermute x7, waiting for transfers between devices, to_x(): return lax.ppermute(value, 'depth', pairs)  12.8 us
    ppermute x6, starting transfers between devices, to_core(): return lax.ppermute(value, 'row', [(0, 1), (1, 0)])  10.2 us
    ppermute x7, starting transfers between devices, to_y(): lax.ppermute(value, 'depth', [(k, (k + SIDE * step) % side) for k in rang...  9.99 us
    ppermute x7, waiting for transfers between devices, to_y(): lax.ppermute(value, 'depth', [(k, (k + SIDE * step) % side) for k in rang...  9.68 us
  transfers between devices with their start and end apart: 31, of which 8 were waited for; matrix products, arithmetic and copies ran while one was open for 0% of the time, Pallas kernels for 29%

profile of v2, /device:TPU:1, one launch (start us, length us, event | category | flops | bytes accessed | tf_op | source)
XLA Modules:
  0.0 151.4 jit_solution(9113799197095888539)
XLA Ops:
  0.6 1.0 pad_maximum_fusion.refs_0_
  1.6 6.9 %collective-permute-start.1 = (bf16[40,2048]{1,0:T(8,128)(2,1)S(1)}, bf16[40,2048]{1,0:T(8,128)(2,1)S(1)}, u32[]{:S(2)}, u32[]{:S(2)}) collective-permute-start(bf16[40,2048]{1,0:T(8,128)(2,1)S(1)} %pad_maximum_fusion.refs_0_), channel_id=1, source_target_pairs={{0,96},{16,112},{32,0},{48,16},{64,32},{80,48},{96,64},{112,80},{1... | collective-permute-start | bytes 491528 | tf_op jit(solution)/shard_map/ppermute | solution.py:24
  8.5 3.1 %collective-permute-start = (bf16[40,2048]{1,0:T(8,128)(2,1)S(1)}, bf16[40,2048]{1,0:T(8,128)(2,1)S(1)}, u32[]{:S(2)}, u32[]{:S(2)}) collective-permute-start(bf16[40,2048]{1,0:T(8,128)(2,1)S(1)} %pad_maximum_fusion.refs_0_), channel_id=1, source_target_pairs={{0,112},{16,0},{32,16},{48,32},{64,48},{80,64},{96,80},{112,96},{1... | collective-permute-start | bytes 491528 | tf_op jit(solution)/shard_map/ppermute | solution.py:24
  11.7 2.3 %collective-permute-done.1.refs_2_ = bf16[40,2048]{1,0:T(8,128)(2,1)S(1)} collective-permute-done((bf16[40,2048]{1,0:T(8,128)(2,1)S(1)}, bf16[40,2048]{1,0:T(8,128)(2,1)S(1)}, u32[]{:S(2)}, u32[]{:S(2)}) %collective-permute-start.1) | collective-permute-done | bytes 163872 | tf_op jit(solution)/shard_map/ppermute | solution.py:24
  13.9 4.1 %collective-permute-start.2 = (bf16[40,2048]{1,0:T(8,128)(2,1)S(1)}, bf16[40,2048]{1,0:T(8,128)(2,1)S(1)}, u32[]{:S(2)}, u32[]{:S(2)}) collective-permute-start(bf16[40,2048]{1,0:T(8,128)(2,1)S(1)} %collective-permute-done.1.refs_2_), channel_id=1, source_target_pairs={{0,112},{16,0},{32,16},{48,32},{64,48},{80,64},{96,80},{112,96},{1... | collective-permute-start | bytes 491528 | tf_op jit(solution)/shard_map/ppermute | solution.py:24
  18.0 1.5 %collective-permute-start.6 = (bf16[40,2048]{1,0:T(8,128)(2,1)S(1)}, bf16[40,2048]{1,0:T(8,128)(2,1)S(1)}, u32[]{:S(2)}, u32[]{:S(2)}) collective-permute-start(bf16[40,2048]{1,0:T(8,128)(2,1)S(1)} %collective-permute-done.3.refs_7_), channel_id=1, source_target_pairs={{0,16},{16,32},{32,48},{48,64},{64,80},{80,96},{96,112},{112,0},{1... | collective-permute-start | bytes 491528 | tf_op jit(solution)/shard_map/ppermute | solution.py:24
  19.6 3.6 %collective-permute-start.5 = (bf16[40,1024]{1,0:T(8,128)(2,1)S(1)}, bf16[40,1024]{1,0:T(8,128)(2,1)S(1)}, u32[]{:S(2)}, u32[]{:S(2)}) collective-permute-start(bf16[40,1024]{1,0:T(8,128)(2,1)S(1)} %slice.9), channel_id=1, source_target_pairs={{0,96},{16,112},{32,0},{48,16},{64,32},{80,48},{96,64},{112,80},{1... | collective-permute-start | bytes 245768 | tf_op jit(solution)/shard_map/ppermute | solution.py:24
  23.3 4.2 %collective-permute-done.4.refs_4_ = bf16[40,1024]{1,0:T(8,128)(2,1)S(1)} collective-permute-done((bf16[40,1024]{1,0:T(8,128)(2,1)S(1)}, bf16[40,1024]{1,0:T(8,128)(2,1)S(1)}, u32[]{:S(2)}, u32[]{:S(2)}) %collective-permute-start.4) | collective-permute-done | bytes 81952 | tf_op jit(solution)/shard_map/ppermute | solution.py:24
  27.5 1.9 %shard_map.92 = (bf16[160,2048]{1,0:T(8,128)(2,1)S(1)}, bf16[160,2048]{1,0:T(8,128)(2,1)S(1)}, bf16[4,160,1024]{2,1,0:T(8,128)(2,1)}, bf16[4,160,512]{2,1,0:T(8,128)(2,1)}) custom-call(bf16[40,2048]{1,0:T(8,128)(2,1)S(1)} %pad_maximum_fusion.refs_0_, bf16[40,2048]{1,0:T(8,128)(2,1)S(1)} %collective-permute-done.refs_1_, ...), custom_call_target="tpu_custom_call" | custom-call | tf_op jit(solution)/shard_map/pallas_call | solution.py:60
  29.4 9.0 %shard_map.94 = f32[160,2688]{1,0:T(8,128)S(1)} custom-call(s32[1]{0:T(128)} %bitcast.1.which, bf16[160,2048]{1,0:T(8,128)(2,1)S(1)} %get-tuple-element.43.feat, bf16[160,2048]{1,0:T(8,128)(2,1)S(1)} %get-tuple-element.44.upst, bf16[2048,1792]{1,0:T(8,128)(2,1)} %gate.5, bf16[2048,1792]{1,0:T(8,128)(2,1)} %up.5, bf16[1792,2048]{1,0:T(8,128)(2,1)} %down.5), custom_call_target="tpu_custom_call" | custom-call | flops 1761607680 | bytes 11010048 | tf_op jit(solution)/shard_map/pallas_call | solution.py:130
  38.4 3.4 %collective-permute-start.8 = (f32[160,2688]{1,0:T(8,128)S(1)}, f32[160,2688]{1,0:T(8,128)}, u32[]{:S(2)}, u32[]{:S(2)}) collective-permute-start(f32[160,2688]{1,0:T(8,128)S(1)} %shard_map.94), channel_id=1, source_target_pairs={{0,128},{128,0},{1,129},{129,1},{2,130},{130,2},{3,131},{131,3},{4... | collective-permute-start | bytes 5160968 | tf_op jit(solution)/shard_map/ppermute | solution.py:38
  41.8 4.3 %all-to-all-start.1 = ((bf16[4,160,1024]{2,1,0:T(8,128)(2,1)}), bf16[4,160,1024]{2,1,0:T(8,128)(2,1)}, u32[]{:S(2)}, u32[]{:S(2)}) async-start(bf16[4,160,1024]{2,1,0:T(8,128)(2,1)} %get-tuple-element.56), calls=%async_computation.1 | async-start | bytes 2621440 | tf_op jit(solution)/shard_map/all_to_all | solution.py:42
  46.1 9.2 %shard_map.93.own = f32[160,2688]{1,0:T(8,128)S(1)} custom-call(s32[1]{0:T(128)} %bitcast.which, bf16[160,2048]{1,0:T(8,128)(2,1)S(1)} %get-tuple-element.43.feat, bf16[160,2048]{1,0:T(8,128)(2,1)S(1)} %get-tuple-element.44.upst, bf16[2048,1792]{1,0:T(8,128)(2,1)} %gate.5, bf16[2048,1792]{1,0:T(8,128)(2,1)} %up.5, bf16[1792,2048]{1,0:T(8,128)(2,1)} %down.5), custom_call_target="tpu_custom_call" | custom-call | flops 1761607680 | bytes 11010048 | tf_op jit(solution)/shard_map/pallas_call | solution.py:130
  55.3 3.0 %shard_map.95 = (bf16[160,1408]{1,0:T(8,128)(2,1)}, bf16[160,1280]{1,0:T(8,128)(2,1)}, bf16[160,2688]{1,0:T(8,128)(2,1)}) custom-call(f32[160,2688]{1,0:T(8,128)S(1)} %shard_map.93.own, f32[160,2688]{1,0:T(8,128)} %collective-permute-done.8.theirs), custom_call_target="tpu_custom_call" | custom-call | tf_op jit(solution)/shard_map/pallas_call | solution.py:60
  58.3 1.7 %collective-permute-start.9 = (bf16[160,1408]{1,0:T(8,128)(2,1)}, bf16[160,1408]{1,0:T(8,128)(2,1)S(1)}, u32[]{:S(2)}, u32[]{:S(2)}) collective-permute-start(bf16[160,1408]{1,0:T(8,128)(2,1)} %get-tuple-element.45.refs_0_), channel_id=1, source_target_pairs={{0,1},{1,2},{2,3},{3,0},{4,5},{5,6},{6,7},{7,4},{8,9},{9,10},{10,1... | collective-permute-start | bytes 1351688 | tf_op jit(solution)/shard_map/ppermute | solution.py:29
  60.0 1.3 collective-permute-start.10
  61.3 1.4 collective-permute-start.13
  62.8 1.2 collective-permute-start.12
  64.2 9.9 %collective-permute-done.9.refs_1_ = bf16[160,1408]{1,0:T(8,128)(2,1)S(1)} collective-permute-done((bf16[160,1408]{1,0:T(8,128)(2,1)}, bf16[160,1408]{1,0:T(8,128)(2,1)S(1)}, u32[]{:S(2)}, u32[]{:S(2)}) %collective-permute-start.9) | collective-permute-done | bytes 450592 | tf_op jit(solution)/shard_map/ppermute | solution.py:29
  74.1 0.5 collective-permute-start.16
  74.5 4.2 %all-to-all-start.2 = ((bf16[4,160,512]{2,1,0:T(8,128)(2,1)}), bf16[4,160,512]{2,1,0:T(8,128)(2,1)S(1)}, u32[]{:S(2)}, u32[]{:S(2)}) async-start(bf16[4,160,512]{2,1,0:T(8,128)(2,1)} %get-tuple-element.68), calls=%async_computation.2 | async-start | bytes 1310720 | tf_op jit(solution)/shard_map/all_to_all | solution.py:42
  78.8 1.5 %collective-permute-start.15 = (bf16[160,1280]{1,0:T(8,128)(2,1)}, bf16[160,1280]{1,0:T(8,128)(2,1)S(1)}, u32[]{:S(2)}, u32[]{:S(2)}) collective-permute-start(bf16[160,1280]{1,0:T(8,128)(2,1)} %collective-permute-done.10.refs_1_), channel_id=1, source_target_pairs={{0,4},{1,5},{2,6},{3,7},{4,8},{5,9},{6,10},{7,11},{8,12},{9,13},{1... | collective-permute-start | bytes 1228808 | tf_op jit(solution)/shard_map/ppermute | solution.py:34
  80.4 0.9 copy-done.1
  81.3 14.8 %shard_map.96 = bf16[8,20,4096]{2,1,0:T(8,128)(2,1)} custom-call(s32[2]{0:T(128)S(1)} %pad_add_fusion.place, bf16[160,2688]{1,0:T(8,128)(2,1)} %get-tuple-element.48.own, bf16[160,2688]{1,0:T(8,128)(2,1)} %copy-done.1, bf16[2048,1792]{1,0:T(8,128)(2,1)} %gate.5, bf16[2048,1792]{1,0:T(8,128)(2,1)} %up.5, bf16[1792,2048]{1,0:T(8,128)(2,1)} %down.5), custom_call_target="tpu_custom_call" | custom-call | flops 3523215360 | bytes 22020096 | tf_op jit(solution)/shard_map/pallas_call | solution.py:206
  96.1 1.9 %collective-permute-done.15.refs_3_ = bf16[160,1280]{1,0:T(8,128)(2,1)S(1)} collective-permute-done((bf16[160,1280]{1,0:T(8,128)(2,1)}, bf16[160,1280]{1,0:T(8,128)(2,1)S(1)}, u32[]{:S(2)}, u32[]{:S(2)}) %collective-permute-start.15) | collective-permute-done | bytes 409632 | tf_op jit(solution)/shard_map/ppermute | solution.py:34
  97.9 0.8 copy-done.4
  98.7 3.7 %all-to-all-start = ((bf16[8,20,4096]{2,1,0:T(8,128)(2,1)}), bf16[8,20,4096]{2,1,0:T(8,128)(2,1)S(1)}, u32[]{:S(2)}, u32[]{:S(2)}) async-start(bf16[8,20,4096]{2,1,0:T(8,128)(2,1)} %shard_map.96), calls=%async_computation | async-start | bytes 3145728 | tf_op jit(solution)/shard_map/all_to_all | solution.py:411
  102.4 1.5 %collective-permute-start.22 = (bf16[4,160,512]{2,1,0:T(8,128)(2,1)S(1)}, bf16[4,160,512]{2,1,0:T(8,128)(2,1)}, u32[]{:S(2)}, u32[]{:S(2)}) collective-permute-start(bf16[4,160,512]{2,1,0:T(8,128)(2,1)S(1)} %all-to-all-done.2.refs_4_), channel_id=1, source_target_pairs={{0,128},{128,0},{1,129},{129,1},{2,130},{130,2},{3,131},{131,3},{4... | collective-permute-start | bytes 1966088 | tf_op jit(solution)/shard_map/ppermute | solution.py:38
  104.0 1.1 copy-done
  105.1 3.1 %shard_map.99 = (bf16[128,1408]{1,0:T(8,128)(2,1)S(1)}, bf16[128,1408]{1,0:T(8,128)(2,1)S(1)}) custom-call(s32[2]{0:T(128)S(1)} %pad_add_fusion.1.place, bf16[160,1408]{1,0:T(8,128)(2,1)} %get-tuple-element.45.refs_0_, bf16[160,1408]{1,0:T(8,128)(2,1)} %copy-done.3, bf16[160,1408]{1,0:T(8,128)(2,1)} %collective-permute-done.12.refs_2_, ...), custom_call_target="tpu_custom_call" | custom-call | flops 922746880 | bytes 2457600 | tf_op jit(solution)/shard_map/pallas_call | solution.py:267
  108.3 2.7 %collective-permute-start.18 = (bf16[128,1408]{1,0:T(8,128)(2,1)S(1)}, bf16[128,1408]{1,0:T(8,128)(2,1)S(1)}, u32[]{:S(2)}, u32[]{:S(2)}) collective-permute-start(bf16[128,1408]{1,0:T(8,128)(2,1)S(1)} %get-tuple-element.61), channel_id=1, source_target_pairs={{0,12},{1,13},{2,14},{3,15},{4,0},{5,1},{6,2},{7,3},{8,4},{9,5},{1... | collective-permute-start | bytes 1081352 | tf_op jit(solution)/shard_map/ppermute | solution.py:34
  111.0 2.9 %shard_map.103 = (bf16[128,1280]{1,0:T(8,128)(2,1)S(1)}, bf16[128,1280]{1,0:T(8,128)(2,1)S(1)}) custom-call(s32[2]{0:T(128)S(1)} %pad_add_fusion.2.place, bf16[160,1280]{1,0:T(8,128)(2,1)} %get-tuple-element.46.refs_0_, bf16[160,1280]{1,0:T(8,128)(2,1)} %collective-permute-done.10.refs_1_, bf16[160,1280]{1,0:T(8,128)(2,1)} %collective-permute-done.13.refs_2_, ...), custom_call_target="tpu_custom_call" | custom-call | flops 838860800 | bytes 1966080 | tf_op jit(solution)/shard_map/pallas_call | solution.py:267
  114.0 2.7 %collective-permute-start.24 = (bf16[128,1280]{1,0:T(8,128)(2,1)S(1)}, bf16[128,1280]{1,0:T(8,128)(2,1)S(1)}, u32[]{:S(2)}, u32[]{:S(2)}) collective-permute-start(bf16[128,1280]{1,0:T(8,128)(2,1)S(1)} %get-tuple-element.73), channel_id=1, source_target_pairs={{0,3},{1,0},{2,1},{3,2},{4,7},{5,4},{6,5},{7,6},{8,11},{9,8},{10,9... | collective-permute-start | bytes 983048 | tf_op jit(solution)/shard_map/ppermute | solution.py:29
  116.7 5.0 %shard_map.98 = (f32[256,1408]{1,0:T(8,128)S(1)}, f32[256,1408]{1,0:T(8,128)S(1)}, f32[256,1408]{1,0:T(8,128)S(1)}) custom-call(s32[2]{0:T(128)S(1)} %pad_add_fusion.1.place, bf16[160,1408]{1,0:T(8,128)(2,1)} %get-tuple-element.45.refs_0_, bf16[160,1408]{1,0:T(8,128)(2,1)} %copy-done.3, bf16[160,1408]{1,0:T(8,128)(2,1)} %collective-permute-done.12.refs_2_, ...), custom_call_target="tpu_custom_call" | custom-call | flops 1384120320 | bytes 3768320 | tf_op jit(solution)/shard_map/pallas_call | solution.py:267
  121.7 0.2 shard_map.100
  121.9 0.3 collective-permute-start.19
  122.2 2.7 %collective-permute-start.20 = (bf16[256,1408]{1,0:T(8,128)(2,1)S(1)}, bf16[256,1408]{1,0:T(8,128)(2,1)S(1)}, u32[]{:S(2)}, u32[]{:S(2)}) collective-permute-start(bf16[256,1408]{1,0:T(8,128)(2,1)S(1)} %get-tuple-element.63), channel_id=1, source_target_pairs={{0,12},{1,13},{2,14},{3,15},{4,0},{5,1},{6,2},{7,3},{8,4},{9,5},{1... | collective-permute-start | bytes 2162696 | tf_op jit(solution)/shard_map/ppermute | solution.py:34
  124.9 4.2 %shard_map.102 = (f32[256,1280]{1,0:T(8,128)S(1)}, f32[256,1280]{1,0:T(8,128)S(1)}, f32[256,1280]{1,0:T(8,128)S(1)}) custom-call(s32[2]{0:T(128)S(1)} %pad_add_fusion.2.place, bf16[160,1280]{1,0:T(8,128)(2,1)} %get-tuple-element.46.refs_0_, bf16[160,1280]{1,0:T(8,128)(2,1)} %collective-permute-done.10.refs_1_, ...), custom_call_target="tpu_custom_call" | custom-call | flops 1258291200 | bytes 2621440 | tf_op jit(solution)/shard_map/pallas_call | solution.py:267
  129.1 0.2 shard_map.104
  129.4 2.7 %collective-permute-start.26 = (bf16[256,1280]{1,0:T(8,128)(2,1)S(1)}, bf16[256,1280]{1,0:T(8,128)(2,1)S(1)}, u32[]{:S(2)}, u32[]{:S(2)}) collective-permute-start(bf16[256,1280]{1,0:T(8,128)(2,1)S(1)} %get-tuple-element.75), channel_id=1, source_target_pairs={{0,3},{1,0},{2,1},{3,2},{4,7},{5,4},{6,5},{7,6},{8,11},{9,8},{10,9... | collective-permute-start | bytes 1966088 | tf_op jit(solution)/shard_map/ppermute | solution.py:29
  132.1 7.8 %collective-permute-done.19.from_before = bf16[256,1408]{1,0:T(8,128)(2,1)S(1)} collective-permute-done((bf16[256,1408]{1,0:T(8,128)(2,1)S(1)}, bf16[256,1408]{1,0:T(8,128)(2,1)S(1)}, u32[]{:S(2)}, u32[]{:S(2)}) %collective-permute-start.19) | collective-permute-done | bytes 720928 | tf_op jit(solution)/shard_map/ppermute | solution.py:34
  139.9 0.3 shard_map.101
  140.1 2.2 %collective-permute-start.21 = (bf16[128,1408]{1,0:T(8,128)(2,1)S(1)}, bf16[128,1408]{1,0:T(8,128)(2,1)S(1)}, u32[]{:S(2)}, u32[]{:S(2)}) collective-permute-start(bf16[128,1408]{1,0:T(8,128)(2,1)S(1)} %get-tuple-element.65), channel_id=1, source_target_pairs={{0,128},{128,0},{1,129},{129,1},{2,130},{130,2},{3,131},{131,3},{4... | collective-permute-start | bytes 1081352 | tf_op jit(solution)/shard_map/ppermute | solution.py:38
  142.3 2.8 %collective-permute-done.25.from_before = bf16[256,1280]{1,0:T(8,128)(2,1)S(1)} collective-permute-done((bf16[256,1280]{1,0:T(8,128)(2,1)S(1)}, bf16[256,1280]{1,0:T(8,128)(2,1)S(1)}, u32[]{:S(2)}, u32[]{:S(2)}) %collective-permute-start.25) | collective-permute-done | bytes 655392 | tf_op jit(solution)/shard_map/ppermute | solution.py:29
  145.3 2.7 %collective-permute-start.27 = (bf16[128,1280]{1,0:T(8,128)(2,1)S(1)}, bf16[128,1280]{1,0:T(8,128)(2,1)S(1)}, u32[]{:S(2)}, u32[]{:S(2)}) collective-permute-start(bf16[128,1280]{1,0:T(8,128)(2,1)S(1)} %get-tuple-element.77), channel_id=1, source_target_pairs={{0,128},{128,0},{1,129},{129,1},{2,130},{130,2},{3,131},{131,3},{4... | collective-permute-start | bytes 983048 | tf_op jit(solution)/shard_map/ppermute | solution.py:38
  148.0 1.3 collective-permute-done.27.other_b
  149.3 1.3 shard_map.106
  150.6 0.9 shard_map.97
  (45 shorter events, 0.9 us)
Async XLA Ops:
  1.6 12.3 %collective-permute-start.1 = (bf16[40,2048]{1,0:T(8,128)(2,1)S(1)}, bf16[40,2048]{1,0:T(8,128)(2,1)S(1)}, u32[]{:S(2)}, u32[]{:S(2)}) collective-permute-start(bf16[40,2048]{1,0:T(8,128)(2,1)S(1)} %pad_maximum_fusion.refs_0_), channel_id=1, source_target_pairs={{0,96},{16,112},{32,0},{48,16},{64,32},{80,48},{96,64},{112,80},{1... | collective-permute-start | bytes 491528 | tf_op jit(solution)/shard_map/ppermute | solution.py:24
  8.5 9.5 %collective-permute-start.3 = (bf16[40,2048]{1,0:T(8,128)(2,1)S(1)}, bf16[40,2048]{1,0:T(8,128)(2,1)S(1)}, u32[]{:S(2)}, u32[]{:S(2)}) collective-permute-start(bf16[40,2048]{1,0:T(8,128)(2,1)S(1)} %pad_maximum_fusion.refs_0_), channel_id=1, source_target_pairs={{0,32},{16,48},{32,64},{48,80},{64,96},{80,112},{96,0},{112,16},{1... | collective-permute-start | bytes 491528 | tf_op jit(solution)/shard_map/ppermute | solution.py:24
  8.5 11.1 %collective-permute-start = (bf16[40,2048]{1,0:T(8,128)(2,1)S(1)}, bf16[40,2048]{1,0:T(8,128)(2,1)S(1)}, u32[]{:S(2)}, u32[]{:S(2)}) collective-permute-start(bf16[40,2048]{1,0:T(8,128)(2,1)S(1)} %pad_maximum_fusion.refs_0_), channel_id=1, source_target_pairs={{0,112},{16,0},{32,16},{48,32},{64,48},{80,64},{96,80},{112,96},{1... | collective-permute-start | bytes 491528 | tf_op jit(solution)/shard_map/ppermute | solution.py:24
  11.7 11.6 %collective-permute-start.7 = (bf16[40,2048]{1,0:T(8,128)(2,1)S(1)}, bf16[40,2048]{1,0:T(8,128)(2,1)S(1)}, u32[]{:S(2)}, u32[]{:S(2)}) collective-permute-start(bf16[40,2048]{1,0:T(8,128)(2,1)S(1)} %pad_maximum_fusion.refs_0_), channel_id=1, source_target_pairs={{0,16},{16,32},{32,48},{48,64},{64,80},{80,96},{96,112},{112,0},{1... | collective-permute-start | bytes 491528 | tf_op jit(solution)/shard_map/ppermute | solution.py:24
  13.9 13.6 %collective-permute-start.2 = (bf16[40,2048]{1,0:T(8,128)(2,1)S(1)}, bf16[40,2048]{1,0:T(8,128)(2,1)S(1)}, u32[]{:S(2)}, u32[]{:S(2)}) collective-permute-start(bf16[40,2048]{1,0:T(8,128)(2,1)S(1)} %collective-permute-done.1.refs_2_), channel_id=1, source_target_pairs={{0,112},{16,0},{32,16},{48,32},{64,48},{80,64},{96,80},{112,96},{1... | collective-permute-start | bytes 491528 | tf_op jit(solution)/shard_map/ppermute | solution.py:24
  18.0 9.4 %collective-permute-start.6 = (bf16[40,2048]{1,0:T(8,128)(2,1)S(1)}, bf16[40,2048]{1,0:T(8,128)(2,1)S(1)}, u32[]{:S(2)}, u32[]{:S(2)}) collective-permute-start(bf16[40,2048]{1,0:T(8,128)(2,1)S(1)} %collective-permute-done.3.refs_7_), channel_id=1, source_target_pairs={{0,16},{16,32},{32,48},{48,64},{64,80},{80,96},{96,112},{112,0},{1... | collective-permute-start | bytes 491528 | tf_op jit(solution)/shard_map/ppermute | solution.py:24
  19.6 7.9 %collective-permute-start.4 = (bf16[40,1024]{1,0:T(8,128)(2,1)S(1)}, bf16[40,1024]{1,0:T(8,128)(2,1)S(1)}, u32[]{:S(2)}, u32[]{:S(2)}) collective-permute-start(bf16[40,1024]{1,0:T(8,128)(2,1)S(1)} %slice.8), channel_id=1, source_target_pairs={{0,32},{16,48},{32,64},{48,80},{64,96},{80,112},{96,0},{112,16},{1... | collective-permute-start | bytes 245768 | tf_op jit(solution)/shard_map/ppermute | solution.py:24
  19.6 7.9 %collective-permute-start.5 = (bf16[40,1024]{1,0:T(8,128)(2,1)S(1)}, bf16[40,1024]{1,0:T(8,128)(2,1)S(1)}, u32[]{:S(2)}, u32[]{:S(2)}) collective-permute-start(bf16[40,1024]{1,0:T(8,128)(2,1)S(1)} %slice.9), channel_id=1, source_target_pairs={{0,96},{16,112},{32,0},{48,16},{64,32},{80,48},{96,64},{112,80},{1... | collective-permute-start | bytes 245768 | tf_op jit(solution)/shard_map/ppermute | solution.py:24
  38.4 16.8 %collective-permute-start.8 = (f32[160,2688]{1,0:T(8,128)S(1)}, f32[160,2688]{1,0:T(8,128)}, u32[]{:S(2)}, u32[]{:S(2)}) collective-permute-start(f32[160,2688]{1,0:T(8,128)S(1)} %shard_map.94), channel_id=1, source_target_pairs={{0,128},{128,0},{1,129},{129,1},{2,130},{130,2},{3,131},{131,3},{4... | collective-permute-start | bytes 5160968 | tf_op jit(solution)/shard_map/ppermute | solution.py:38
  41.8 22.4 %all-to-all-start.1 = ((bf16[4,160,1024]{2,1,0:T(8,128)(2,1)}), bf16[4,160,1024]{2,1,0:T(8,128)(2,1)}, u32[]{:S(2)}, u32[]{:S(2)}) async-start(bf16[4,160,1024]{2,1,0:T(8,128)(2,1)} %get-tuple-element.56), calls=%async_computation.1 | async-start | bytes 2621440 | tf_op jit(solution)/shard_map/all_to_all | solution.py:42
  58.3 22.1 %collective-permute-start.11 = (bf16[160,2688]{1,0:T(8,128)(2,1)}, bf16[160,2688]{1,0:T(8,128)(2,1)S(1)}, u32[]{:S(2)}, u32[]{:S(2)}) collective-permute-start(bf16[160,2688]{1,0:T(8,128)(2,1)} %get-tuple-element.48.own), channel_id=1, source_target_pairs={{0,128},{128,0},{1,129},{129,1},{2,130},{130,2},{3,131},{131,3},{4... | collective-permute-start | bytes 2580488 | tf_op jit(solution)/shard_map/ppermute | solution.py:38
  58.3 15.7 %collective-permute-start.9 = (bf16[160,1408]{1,0:T(8,128)(2,1)}, bf16[160,1408]{1,0:T(8,128)(2,1)S(1)}, u32[]{:S(2)}, u32[]{:S(2)}) collective-permute-start(bf16[160,1408]{1,0:T(8,128)(2,1)} %get-tuple-element.45.refs_0_), channel_id=1, source_target_pairs={{0,1},{1,2},{2,3},{3,0},{4,5},{5,6},{6,7},{7,4},{8,9},{9,10},{10,1... | collective-permute-start | bytes 1351688 | tf_op jit(solution)/shard_map/ppermute | solution.py:29
  60.0 18.7 %collective-permute-start.10 = (bf16[160,1280]{1,0:T(8,128)(2,1)}, bf16[160,1280]{1,0:T(8,128)(2,1)}, u32[]{:S(2)}, u32[]{:S(2)}) collective-permute-start(bf16[160,1280]{1,0:T(8,128)(2,1)} %get-tuple-element.46.refs_0_), channel_id=1, source_target_pairs={{0,4},{1,5},{2,6},{3,7},{4,8},{5,9},{6,10},{7,11},{8,12},{9,13},{1... | collective-permute-start | bytes 1228808 | tf_op jit(solution)/shard_map/ppermute | solution.py:34
  61.3 17.4 %collective-permute-start.13 = (bf16[160,1280]{1,0:T(8,128)(2,1)}, bf16[160,1280]{1,0:T(8,128)(2,1)}, u32[]{:S(2)}, u32[]{:S(2)}) collective-permute-start(bf16[160,1280]{1,0:T(8,128)(2,1)} %get-tuple-element.46.refs_0_), channel_id=1, source_target_pairs={{0,12},{1,13},{2,14},{3,15},{4,0},{5,1},{6,2},{7,3},{8,4},{9,5},{1... | collective-permute-start | bytes 1228808 | tf_op jit(solution)/shard_map/ppermute | solution.py:34
  62.8 17.6 %collective-permute-start.12 = (bf16[160,1408]{1,0:T(8,128)(2,1)}, bf16[160,1408]{1,0:T(8,128)(2,1)}, u32[]{:S(2)}, u32[]{:S(2)}) collective-permute-start(bf16[160,1408]{1,0:T(8,128)(2,1)} %get-tuple-element.45.refs_0_), channel_id=1, source_target_pairs={{0,3},{1,0},{2,1},{3,2},{4,7},{5,4},{6,5},{7,6},{8,11},{9,8},{10,9... | collective-permute-start | bytes 1351688 | tf_op jit(solution)/shard_map/ppermute | solution.py:29
  74.1 22.0 %copy-start.3 = (bf16[160,1408]{1,0:T(8,128)(2,1)}, bf16[160,1408]{1,0:T(8,128)(2,1)S(1)}, u32[]{:S(2)}) copy-start(bf16[160,1408]{1,0:T(8,128)(2,1)S(1)} %collective-permute-done.9.refs_1_) | copy-start | bytes 1351684
  74.1 29.9 %collective-permute-start.16 = (bf16[4,160,1024]{2,1,0:T(8,128)(2,1)}, bf16[4,160,1024]{2,1,0:T(8,128)(2,1)S(1)}, u32[]{:S(2)}, u32[]{:S(2)}) collective-permute-start(bf16[4,160,1024]{2,1,0:T(8,128)(2,1)} %all-to-all-done.1.refs_4_), channel_id=1, source_target_pairs={{0,128},{128,0},{1,129},{129,1},{2,130},{130,2},{3,131},{131,3},{4... | collective-permute-start | bytes 3932168 | tf_op jit(solution)/shard_map/ppermute | solution.py:38
  74.5 24.1 %all-to-all-start.2 = ((bf16[4,160,512]{2,1,0:T(8,128)(2,1)}), bf16[4,160,512]{2,1,0:T(8,128)(2,1)S(1)}, u32[]{:S(2)}, u32[]{:S(2)}) async-start(bf16[4,160,512]{2,1,0:T(8,128)(2,1)} %get-tuple-element.68), calls=%async_computation.2 | async-start | bytes 1310720 | tf_op jit(solution)/shard_map/all_to_all | solution.py:42
  78.7 19.9 %collective-permute-start.14 = (bf16[160,1408]{1,0:T(8,128)(2,1)S(1)}, bf16[160,1408]{1,0:T(8,128)(2,1)}, u32[]{:S(2)}, u32[]{:S(2)}) collective-permute-start(bf16[160,1408]{1,0:T(8,128)(2,1)S(1)} %collective-permute-done.9.refs_1_), channel_id=1, source_target_pairs={{0,1},{1,2},{2,3},{3,0},{4,5},{5,6},{6,7},{7,4},{8,9},{9,10},{10,1... | collective-permute-start | bytes 1351688 | tf_op jit(solution)/shard_map/ppermute | solution.py:29
  78.8 19.1 %collective-permute-start.15 = (bf16[160,1280]{1,0:T(8,128)(2,1)}, bf16[160,1280]{1,0:T(8,128)(2,1)S(1)}, u32[]{:S(2)}, u32[]{:S(2)}) collective-permute-start(bf16[160,1280]{1,0:T(8,128)(2,1)} %collective-permute-done.10.refs_1_), channel_id=1, source_target_pairs={{0,4},{1,5},{2,6},{3,7},{4,8},{5,9},{6,10},{7,11},{8,12},{9,13},{1... | collective-permute-start | bytes 1228808 | tf_op jit(solution)/shard_map/ppermute | solution.py:34
  80.4 0.9 copy-start.1
  97.9 0.8 copy-start.4
  98.7 3.7 %copy-start.2 = (bf16[4,160,512]{2,1,0:T(8,128)(2,1)}, bf16[4,160,512]{2,1,0:T(8,128)(2,1)S(1)}, u32[]{:S(2)}) copy-start(bf16[4,160,512]{2,1,0:T(8,128)(2,1)S(1)} %all-to-all-done.2.refs_4_) | copy-start | bytes 1966084
  98.7 51.9 %all-to-all-start = ((bf16[8,20,4096]{2,1,0:T(8,128)(2,1)}), bf16[8,20,4096]{2,1,0:T(8,128)(2,1)S(1)}, u32[]{:S(2)}, u32[]{:S(2)}) async-start(bf16[8,20,4096]{2,1,0:T(8,128)(2,1)} %shard_map.96), calls=%async_computation | async-start | bytes 3145728 | tf_op jit(solution)/shard_map/all_to_all | solution.py:411
  102.4 8.7 %collective-permute-start.22 = (bf16[4,160,512]{2,1,0:T(8,128)(2,1)S(1)}, bf16[4,160,512]{2,1,0:T(8,128)(2,1)}, u32[]{:S(2)}, u32[]{:S(2)}) collective-permute-start(bf16[4,160,512]{2,1,0:T(8,128)(2,1)S(1)} %all-to-all-done.2.refs_4_), channel_id=1, source_target_pairs={{0,128},{128,0},{1,129},{129,1},{2,130},{130,2},{3,131},{131,3},{4... | collective-permute-start | bytes 1966088 | tf_op jit(solution)/shard_map/ppermute | solution.py:38
  104.0 1.1 copy-start
  108.2 13.4 %collective-permute-start.17 = (bf16[128,1408]{1,0:T(8,128)(2,1)S(1)}, bf16[128,1408]{1,0:T(8,128)(2,1)S(1)}, u32[]{:S(2)}, u32[]{:S(2)}) collective-permute-start(bf16[128,1408]{1,0:T(8,128)(2,1)S(1)} %get-tuple-element.60), channel_id=1, source_target_pairs={{0,4},{1,5},{2,6},{3,7},{4,8},{5,9},{6,10},{7,11},{8,12},{9,13},{1... | collective-permute-start | bytes 1081352 | tf_op jit(solution)/shard_map/ppermute | solution.py:34
  108.3 13.4 %collective-permute-start.18 = (bf16[128,1408]{1,0:T(8,128)(2,1)S(1)}, bf16[128,1408]{1,0:T(8,128)(2,1)S(1)}, u32[]{:S(2)}, u32[]{:S(2)}) collective-permute-start(bf16[128,1408]{1,0:T(8,128)(2,1)S(1)} %get-tuple-element.61), channel_id=1, source_target_pairs={{0,12},{1,13},{2,14},{3,15},{4,0},{5,1},{6,2},{7,3},{8,4},{9,5},{1... | collective-permute-start | bytes 1081352 | tf_op jit(solution)/shard_map/ppermute | solution.py:34
  113.9 15.2 %collective-permute-start.23 = (bf16[128,1280]{1,0:T(8,128)(2,1)S(1)}, bf16[128,1280]{1,0:T(8,128)(2,1)S(1)}, u32[]{:S(2)}, u32[]{:S(2)}) collective-permute-start(bf16[128,1280]{1,0:T(8,128)(2,1)S(1)} %get-tuple-element.72), channel_id=1, source_target_pairs={{0,1},{1,2},{2,3},{3,0},{4,5},{5,6},{6,7},{7,4},{8,9},{9,10},{10,1... | collective-permute-start | bytes 983048 | tf_op jit(solution)/shard_map/ppermute | solution.py:29
  114.0 15.1 %collective-permute-start.24 = (bf16[128,1280]{1,0:T(8,128)(2,1)S(1)}, bf16[128,1280]{1,0:T(8,128)(2,1)S(1)}, u32[]{:S(2)}, u32[]{:S(2)}) collective-permute-start(bf16[128,1280]{1,0:T(8,128)(2,1)S(1)} %get-tuple-element.73), channel_id=1, source_target_pairs={{0,3},{1,0},{2,1},{3,2},{4,7},{5,4},{6,5},{7,6},{8,11},{9,8},{10,9... | collective-permute-start | bytes 983048 | tf_op jit(solution)/shard_map/ppermute | solution.py:29
  121.9 18.0 %collective-permute-start.19 = (bf16[256,1408]{1,0:T(8,128)(2,1)S(1)}, bf16[256,1408]{1,0:T(8,128)(2,1)S(1)}, u32[]{:S(2)}, u32[]{:S(2)}) collective-permute-start(bf16[256,1408]{1,0:T(8,128)(2,1)S(1)} %get-tuple-element.62), channel_id=1, source_target_pairs={{0,4},{1,5},{2,6},{3,7},{4,8},{5,9},{6,10},{7,11},{8,12},{9,13},{1... | collective-permute-start | bytes 2162696 | tf_op jit(solution)/shard_map/ppermute | solution.py:34
  122.2 17.7 %collective-permute-start.20 = (bf16[256,1408]{1,0:T(8,128)(2,1)S(1)}, bf16[256,1408]{1,0:T(8,128)(2,1)S(1)}, u32[]{:S(2)}, u32[]{:S(2)}) collective-permute-start(bf16[256,1408]{1,0:T(8,128)(2,1)S(1)} %get-tuple-element.63), channel_id=1, source_target_pairs={{0,12},{1,13},{2,14},{3,15},{4,0},{5,1},{6,2},{7,3},{8,4},{9,5},{1... | collective-permute-start | bytes 2162696 | tf_op jit(solution)/shard_map/ppermute | solution.py:34
  129.3 15.8 %collective-permute-start.25 = (bf16[256,1280]{1,0:T(8,128)(2,1)S(1)}, bf16[256,1280]{1,0:T(8,128)(2,1)S(1)}, u32[]{:S(2)}, u32[]{:S(2)}) collective-permute-start(bf16[256,1280]{1,0:T(8,128)(2,1)S(1)} %get-tuple-element.74), channel_id=1, source_target_pairs={{0,1},{1,2},{2,3},{3,0},{4,5},{5,6},{6,7},{7,4},{8,9},{9,10},{10,1... | collective-permute-start | bytes 1966088 | tf_op jit(solution)/shard_map/ppermute | solution.py:29
  129.4 15.7 %collective-permute-start.26 = (bf16[256,1280]{1,0:T(8,128)(2,1)S(1)}, bf16[256,1280]{1,0:T(8,128)(2,1)S(1)}, u32[]{:S(2)}, u32[]{:S(2)}) collective-permute-start(bf16[256,1280]{1,0:T(8,128)(2,1)S(1)} %get-tuple-element.75), channel_id=1, source_target_pairs={{0,3},{1,0},{2,1},{3,2},{4,7},{5,4},{6,5},{7,6},{8,11},{9,8},{10,9... | collective-permute-start | bytes 1966088 | tf_op jit(solution)/shard_map/ppermute | solution.py:29
  140.1 7.9 %collective-permute-start.21 = (bf16[128,1408]{1,0:T(8,128)(2,1)S(1)}, bf16[128,1408]{1,0:T(8,128)(2,1)S(1)}, u32[]{:S(2)}, u32[]{:S(2)}) collective-permute-start(bf16[128,1408]{1,0:T(8,128)(2,1)S(1)} %get-tuple-element.65), channel_id=1, source_target_pairs={{0,128},{128,0},{1,129},{129,1},{2,130},{130,2},{3,131},{131,3},{4... | collective-permute-start | bytes 1081352 | tf_op jit(solution)/shard_map/ppermute | solution.py:38
  145.3 4.0 %collective-permute-start.27 = (bf16[128,1280]{1,0:T(8,128)(2,1)S(1)}, bf16[128,1280]{1,0:T(8,128)(2,1)S(1)}, u32[]{:S(2)}, u32[]{:S(2)}) collective-permute-start(bf16[128,1280]{1,0:T(8,128)(2,1)S(1)} %get-tuple-element.77), channel_id=1, source_target_pairs={{0,128},{128,0},{1,129},{129,1},{2,130},{130,2},{3,131},{131,3},{4... | collective-permute-start | bytes 983048 | tf_op jit(solution)/shard_map/ppermute | solution.py:38
